TPU v7x, 32 devices: a whole 2x2x4 slice. The times are simulated.
32 devices in a mesh: rep: 4 (over y, x), exp: 8 (over z, core).
Axes of the slice: x: 2, y: 2, z: 4, core: 2. Of those that a mesh axis runs over, the one named last changes fastest.
Arguments:
- tokens: bfloat16 [8, 1024, 1024], P('exp', 'rep'), may hold values from -6 to 6
- doc_ids: int32 [8, 1024], P('exp'), may hold values from 0 to 3, as said below
- routes: int32 [8, 1024, 1], P('exp', 'rep'), may hold values from 0 to 3; in each aligned block of 256 rows (0 to 255, 256 to 511, ..., all dimensions but the last counted through in order) at most 80 rows name the same one
- norm_gains: bfloat16 [1024, 2], P(('rep', 'exp')), may hold values from 0.5 to 1.5
- norm_biases: bfloat16 [1024, 2], P(('rep', 'exp')), may hold values from -1 to 1
- w_qkv: bfloat16 [1024, 3072], P(('rep', 'exp')), may hold values from -0.1875 to 0.1875
- w_proj: bfloat16 [1024, 1024], P(('rep', 'exp')), may hold values from -1 to 1
- centroids: bfloat16 [1024, 4], P(('rep', 'exp')), may hold values from -0.1875 to 0.1875
- w_in: bfloat16 [8, 2, 1024, 2048], P('exp', None, None, 'rep'), may hold values from -0.1875 to 0.1875
- w_out: bfloat16 [8, 2, 1024, 2048], P('exp', None, None, 'rep'), may hold values from -0.09375 to 0.09375
- grad_out: bfloat16 [8, 1024, 1024], P('exp', 'rep'), may hold values from -6 to 6
Outputs:
- block_out: bfloat16 [8, 1024, 1024], P('exp', 'rep')
- grad_tokens: bfloat16 [8, 1024, 1024], P('exp', 'rep')
- grad_gains: float32 [1024, 2], P(('rep', 'exp'))
- grad_biases: float32 [1024, 2], P(('rep', 'exp'))
- grad_qkv: float32 [1024, 3072], P(('rep', 'exp'))
- grad_proj: float32 [1024, 1024], P(('rep', 'exp'))
- grad_centroids: float32 [1024, 4], P(('rep', 'exp'))
- grad_w_in: float32 [8, 2, 1024, 2048], P('exp', None, None, 'rep')
- grad_w_out: float32 [8, 2, 1024, 2048], P('exp', None, None, 'rep')
Inputs may be any that keep to these rules, and one draw needn't show every extreme that they name: `routes`: each token names one expert. In the rows of one device no expert is named by more than 80 rows, and in some device's rows one expert by exactly 80. `doc_ids`: within a sequence document numbers start at 0, never fall and rise by one at each boundary; every sequence has one document that starts within its first 128 positions and ends within its last 128.
All inputs are finite; a program needn't handle non-finite values.
Results may differ from a plain program's by a relative error of at most 0.015.
Values may be sent and summed in bfloat16 or wider, within the bound.
No kernel may reach another device: no remote copies, remote signals or barrier semaphores. Data moves between devices by JAX's collectives and lax.ppermute only.
A program may use at most 256 MiB of HBM per device.

v0:
```python
import jax
import jax.numpy as jnp
from jax import lax
from jax.sharding import PartitionSpec as P

HEAD_DIM = 64


eps = 1e-05
neg_fill = -1e30


def from_partner(value, axis, stride):
    mask = 2**stride
    pairs = [(source, source ^ mask) for source in range(lax.axis_size(axis))]
    return lax.ppermute(value, axis, pairs)


def layer_norm(values, gain_vec, shift):
    average = jnp.mean(values, axis=-1, keepdims=True)
    centred = values - average
    inverse = lax.rsqrt(jnp.mean(centred * centred, axis=-1, keepdims=True) + eps)
    normed = centred * inverse
    return (normed * gain_vec + shift, normed, inverse)


def norm_back(gradient, normed, inverse, gain_vec):
    scaled = gradient * gain_vec
    bracket = (
        scaled
        - jnp.mean(scaled, axis=-1, keepdims=True)
        - normed * jnp.mean(scaled * normed, axis=-1, keepdims=True)
    )
    return (inverse * bracket, jnp.sum(gradient * normed, axis=0), jnp.sum(gradient, axis=0))


def slot_table(expert, experts, capacity):
    tok_rows = expert.shape[0]
    onehot = (expert[:, None] == jnp.arange(experts, dtype=jnp.int32)[None, :]).astype(jnp.int32)
    before = jnp.cumsum(onehot, axis=0) - onehot
    slot_rank = jnp.sum(before * onehot, axis=1)
    slot_of = expert * capacity + slot_rank % 2 * (capacity // 2) + slot_rank // 2
    slot_owner = jnp.full((experts * capacity,), tok_rows, jnp.int32)
    slot_owner = slot_owner.at[slot_of].set(jnp.arange(tok_rows, dtype=jnp.int32))
    return (slot_of, slot_owner)


def pack_rows(values, slot_owner, experts, capacity):
    padded = jnp.concatenate([values, jnp.zeros((1, values.shape[1]), values.dtype)], axis=0)
    return padded[slot_owner].reshape(experts, capacity, values.shape[1])


def own_half(block, parity):
    split = block.reshape(block.shape[0], 2, block.shape[1] // 2, block.shape[2])
    return lax.dynamic_index_in_dim(split, parity, axis=1, keepdims=False)


def contract_rows(former, latter):
    return lax.dot_general(
        former, latter, (((0,), (0,)), ((), ())), preferred_element_type=jnp.float32
    )


def contract_last(former, latter):
    return lax.dot_general(
        former, latter, (((1,), (1,)), ((), ())), preferred_element_type=jnp.float32
    )


def pair_total(partial_sum):
    return partial_sum + from_partner(partial_sum.astype(jnp.bfloat16), "exp", 0).astype(
        partial_sum.dtype
    )


def expert_states(inputs, expert_in, expert_out):
    stream = inputs.astype(jnp.float32)
    stored = []
    for sublayer in range(2):
        stream_b = stream.astype(jnp.bfloat16)
        pre_act = jnp.dot(stream_b, expert_in[sublayer], preferred_element_type=jnp.float32)
        active = jax.nn.gelu(pre_act).astype(jnp.bfloat16)
        stream = stream + pair_total(contract_last(active, expert_out[sublayer]))
        stored.append((stream_b, pre_act, active))
    return (stream, stored)


def gating_of(inputs, centroid):
    return jax.nn.sigmoid(jnp.dot(inputs, centroid, preferred_element_type=jnp.float32))


def layer_back(grad_stream, stored_layer, in_layer, out_layer):
    stream_b, pre_act, active = stored_layer
    grad_branch = grad_stream.astype(jnp.bfloat16)
    grad_out_layer = contract_rows(grad_branch, active)
    grad_active = jnp.dot(grad_branch, out_layer, preferred_element_type=jnp.float32)
    unused, gelu_back = jax.vjp(jax.nn.gelu, pre_act)
    grad_pre = gelu_back(grad_active)[0].astype(jnp.bfloat16)
    grad_in_layer = contract_rows(stream_b, grad_pre)
    grad_stream = grad_stream + pair_total(contract_last(grad_pre, in_layer))
    return (grad_stream, grad_in_layer, grad_out_layer)


def local(
    tokens,
    doc_ids,
    routes,
    norm_gains,
    norm_biases,
    w_qkv,
    w_proj,
    centroids,
    w_in,
    w_out,
    grad_out,
):
    tok_rows = tokens.shape[1]
    model_width = tokens.shape[2]
    seq_len = doc_ids.shape[1]
    experts = lax.axis_size("exp") // 2
    capacity = 2 * (5 * tok_rows // (8 * experts))
    head_count = model_width // HEAD_DIM
    score_scale = HEAD_DIM ** (-0.5)
    parity = lax.axis_index("exp") % 2
    own_expert = lax.axis_index("exp") // 2
    qkv_full, proj_full, gain_full, bias_full, cent_full = (
        lax.all_gather(w_qkv, ("rep", "exp"), axis=0, tiled=True),
        lax.all_gather(w_proj, ("rep", "exp"), axis=0, tiled=True),
        lax.all_gather(norm_gains, ("rep", "exp"), axis=0, tiled=True),
        lax.all_gather(norm_biases, ("rep", "exp"), axis=0, tiled=True),
        lax.all_gather(centroids, ("rep", "exp"), axis=0, tiled=True),
    )
    gains = gain_full.astype(jnp.float32)
    biases = bias_full.astype(jnp.float32)
    centroid = lax.dynamic_slice_in_dim(cent_full, own_expert, 1, 1)[:, 0]
    in_half, out_half = (
        lax.all_gather(w_in, "rep", axis=3, tiled=True),
        lax.all_gather(w_out, "rep", axis=3, tiled=True),
    )
    expert_in = in_half[0]
    expert_out = out_half[0]
    tokens32 = tokens[0].astype(jnp.float32)
    normed_in, unit_in, inverse_in = layer_norm(tokens32, gains[:, 0], biases[:, 0])
    attn_in = normed_in.astype(jnp.bfloat16)
    projected = jnp.dot(attn_in, qkv_full, preferred_element_type=jnp.float32).astype(jnp.bfloat16)
    query = projected[:, :model_width].reshape(tok_rows, head_count, HEAD_DIM)
    kv_all = lax.all_gather(projected[:, model_width:], "rep", axis=0, tiled=True)
    keys = kv_all[:, :model_width].reshape(seq_len, head_count, HEAD_DIM)
    values = kv_all[:, model_width:].reshape(seq_len, head_count, HEAD_DIM)
    doc_row = doc_ids[0]
    start_row = lax.axis_index("rep") * tok_rows
    query_pos = start_row + jnp.arange(tok_rows)
    key_pos = jnp.arange(seq_len)
    query_doc = lax.dynamic_slice_in_dim(doc_row, start_row, tok_rows)
    allowed = (key_pos[None, :] <= query_pos[:, None]) & (doc_row[None, :] == query_doc[:, None])

    def scores_of():
        raw = (
            jnp.einsum("qhd,khd->hqk", query, keys, preferred_element_type=jnp.float32)
            * score_scale
        )
        return jnp.where(allowed[None], raw, neg_fill)

    scores = scores_of()
    row_max = jnp.max(scores, axis=-1, keepdims=True)
    exponent = jnp.exp(scores - row_max)
    row_total = jnp.sum(exponent, axis=-1, keepdims=True)
    probs = exponent / row_total
    log_total = row_max + jnp.log(row_total)
    mixed = jnp.einsum(
        "hqk,khd->qhd", probs.astype(jnp.bfloat16), values, preferred_element_type=jnp.float32
    )
    mixed = mixed.reshape(tok_rows, model_width).astype(jnp.bfloat16)
    hidden = tokens32 + jnp.dot(mixed, proj_full, preferred_element_type=jnp.float32)
    normed_mid, unit_mid, inverse_mid = layer_norm(hidden, gains[:, 1], biases[:, 1])
    expert_inputs = normed_mid.astype(jnp.bfloat16)
    slot_of, slot_owner = slot_table(routes[0, :, 0], experts, capacity)
    send_rows = jnp.repeat(pack_rows(expert_inputs, slot_owner, experts, capacity), 2, axis=0)
    received = lax.all_to_all(send_rows, "exp", split_axis=0, concat_axis=0, tiled=True)
    recv_flat = received.reshape(-1, model_width)
    final, unused_store = expert_states(recv_flat, expert_in, expert_out)
    gating = gating_of(recv_flat, centroid)
    answer = (gating[:, None] * final).astype(jnp.bfloat16).reshape(received.shape)
    returned = lax.all_to_all(
        own_half(answer, parity), "exp", split_axis=0, concat_axis=0, tiled=True
    )
    combined = returned.reshape(-1, model_width)[slot_of].astype(jnp.float32)
    block_out = (hidden + combined).astype(jnp.bfloat16)
    send_grad = jnp.repeat(pack_rows(grad_out[0], slot_owner, experts, capacity), 2, axis=0)
    again, grad_recv = (
        lax.all_to_all(send_rows, "exp", split_axis=0, concat_axis=0, tiled=True),
        lax.all_to_all(send_grad, "exp", split_axis=0, concat_axis=0, tiled=True),
    )
    rows_back = again.reshape(-1, model_width)
    grad_rows = grad_recv.reshape(-1, model_width).astype(jnp.float32)
    final, stored = expert_states(rows_back, expert_in, expert_out)
    gating = gating_of(rows_back, centroid)
    grad_score = jnp.sum(grad_rows * final, axis=-1) * gating * (1.0 - gating)
    grad_centroid = jnp.sum(grad_score[:, None] * rows_back.astype(jnp.float32), axis=0)
    feature_half = jnp.arange(model_width) // (model_width // 2) == parity
    column_mask = jnp.arange(cent_full.shape[1]) == own_expert
    grad_cent_mat = jnp.where(
        feature_half[:, None] & column_mask[None, :], grad_centroid[:, None], 0.0
    )
    grad_stream = gating[:, None] * grad_rows
    grad_stream, in_late, out_late = layer_back(grad_stream, stored[1], expert_in[1], expert_out[1])
    grad_stream, in_early, out_early = layer_back(
        grad_stream, stored[0], expert_in[0], expert_out[0]
    )
    grad_w_in, grad_w_out = (
        lax.psum_scatter(
            jnp.stack([in_early, in_late])[None].astype(jnp.bfloat16),
            "rep",
            scatter_dimension=3,
            tiled=True,
        ).astype(jnp.float32),
        lax.psum_scatter(
            jnp.stack([out_early, out_late])[None].astype(jnp.bfloat16),
            "rep",
            scatter_dimension=3,
            tiled=True,
        ).astype(jnp.float32),
    )
    grad_inputs = (grad_stream + grad_score[:, None] * centroid.astype(jnp.float32)).astype(
        jnp.bfloat16
    )
    grad_back = lax.all_to_all(
        own_half(grad_inputs.reshape(received.shape), parity),
        "exp",
        split_axis=0,
        concat_axis=0,
        tiled=True,
    )
    grad_mid = grad_back.reshape(-1, model_width)[slot_of].astype(jnp.float32)
    grad_mid_in, grad_gain_mid, grad_bias_mid = norm_back(
        grad_mid, unit_mid, inverse_mid, gains[:, 1]
    )
    grad_hidden = grad_out[0].astype(jnp.float32) + grad_mid_in
    grad_hidden_b = grad_hidden.astype(jnp.bfloat16)
    grad_proj = contract_rows(mixed, grad_hidden_b)
    grad_mixed = (
        contract_last(grad_hidden_b, proj_full)
        .astype(jnp.bfloat16)
        .reshape(tok_rows, head_count, HEAD_DIM)
    )
    scores = scores_of()
    probs = jnp.exp(scores - log_total)
    grad_values = jnp.einsum(
        "hqk,qhd->khd", probs.astype(jnp.bfloat16), grad_mixed, preferred_element_type=jnp.float32
    )
    grad_probs = jnp.einsum("qhd,khd->hqk", grad_mixed, values, preferred_element_type=jnp.float32)
    grad_scores = (
        probs * (grad_probs - jnp.sum(grad_probs * probs, axis=-1, keepdims=True))
    ).astype(jnp.bfloat16)
    grad_query = (
        jnp.einsum("hqk,khd->qhd", grad_scores, keys, preferred_element_type=jnp.float32)
        * score_scale
    )
    grad_keys = (
        jnp.einsum("hqk,qhd->khd", grad_scores, query, preferred_element_type=jnp.float32)
        * score_scale
    )
    key_part, value_part = (
        lax.psum_scatter(
            grad_keys.reshape(seq_len, model_width).astype(jnp.bfloat16),
            "rep",
            scatter_dimension=0,
            tiled=True,
        ).astype(jnp.float32),
        lax.psum_scatter(
            grad_values.reshape(seq_len, model_width).astype(jnp.bfloat16),
            "rep",
            scatter_dimension=0,
            tiled=True,
        ).astype(jnp.float32),
    )
    grad_projected = jnp.concatenate(
        [grad_query.reshape(tok_rows, model_width), key_part, value_part], axis=1
    ).astype(jnp.bfloat16)
    grad_qkv = contract_rows(attn_in, grad_projected)
    grad_attn_in = contract_last(grad_projected, qkv_full)
    grad_first, grad_gain_in, grad_bias_in = norm_back(
        grad_attn_in, unit_in, inverse_in, gains[:, 0]
    )
    grad_tokens = (grad_hidden + grad_first).astype(jnp.bfloat16)
    sum_qkv, sum_proj, sum_gain, sum_bias, sum_cent = (
        lax.psum_scatter(grad_qkv, ("rep", "exp"), scatter_dimension=0, tiled=True),
        lax.psum_scatter(grad_proj, ("rep", "exp"), scatter_dimension=0, tiled=True),
        lax.psum_scatter(
            jnp.stack([grad_gain_in, grad_gain_mid], axis=1),
            ("rep", "exp"),
            scatter_dimension=0,
            tiled=True,
        ),
        lax.psum_scatter(
            jnp.stack([grad_bias_in, grad_bias_mid], axis=1),
            ("rep", "exp"),
            scatter_dimension=0,
            tiled=True,
        ),
        lax.psum_scatter(grad_cent_mat, ("rep", "exp"), scatter_dimension=0, tiled=True),
    )
    return (
        block_out.reshape(1, tok_rows, model_width),
        grad_tokens.reshape(1, tok_rows, model_width),
        sum_gain,
        sum_bias,
        sum_qkv,
        sum_proj,
        sum_cent,
        grad_w_in,
        grad_w_out,
    )


def solution(mesh):
    in_specs = (
        P("exp", "rep", None),
        P("exp", None),
        P("exp", "rep", None),
        P(("rep", "exp"), None),
        P(("rep", "exp"), None),
        P(("rep", "exp"), None),
        P(("rep", "exp"), None),
        P(("rep", "exp"), None),
        P("exp", None, None, "rep"),
        P("exp", None, None, "rep"),
        P("exp", "rep", None),
    )
    out_specs = (
        P("exp", "rep", None),
        P("exp", "rep", None),
        P(("rep", "exp"), None),
        P(("rep", "exp"), None),
        P(("rep", "exp"), None),
        P(("rep", "exp"), None),
        P(("rep", "exp"), None),
        P("exp", None, None, "rep"),
        P("exp", None, None, "rep"),
    )
    return jax.shard_map(local, mesh=mesh, in_specs=in_specs, out_specs=out_specs, check_vma=False)
```

profile of v0, /device:TPU:0, one launch (start us, length us, event | category | flops | bytes accessed | tf_op | source)
XLA Modules:
  0.0 1539.6 jit_solution(10821953144010198213)
XLA Ops:
  8.0 43.2 %all-gather = bf16[32,32,2]{1,2,0:T(2,128)(2,1)S(1)} all-gather(bf16[1,32,2]{1,2,0:T(2,128)(2,1)} %bitcast.252), channel_id=1, replica_groups=mesh['rep'=4,'exp'=8] {'rep','exp'}, dimensions={0}, use_global_device_ids=true | all-gather | bytes 4224 | tf_op jit(solution)/shard_map/all_gather | solution.py:129
  51.3 36.8 %all-gather.1 = bf16[32,32,2]{1,2,0:T(2,128)(2,1)S(1)} all-gather(bf16[1,32,2]{1,2,0:T(2,128)(2,1)} %bitcast.253), channel_id=1, replica_groups=mesh['rep'=4,'exp'=8] {'rep','exp'}, dimensions={0}, use_global_device_ids=true | all-gather | bytes 4224 | tf_op jit(solution)/shard_map/all_gather | solution.py:130
  90.8 4.9 convolution_convert_fusion
  102.7 44.5 %all-gather.11.cloned.1.call-done = bf16[1024,2048]{1,0:T(8,128)(2,1)} async-done(((bf16[256,2048]{1,0:T(8,128)(2,1)}), bf16[1024,2048]{1,0:T(8,128)(2,1)}) %all-gather.11.cloned.1.call-update) | async-done | bytes 4194320 | tf_op jit(solution)/shard_map/all_gather | solution.py:147
  147.3 4.7 fusion.90
  151.9 2.9 copy.52
  154.8 4.6 copy.50
  159.4 3.0 fusion.93
  162.5 3.8 fusion
  166.3 2.4 copy-done
  168.8 4.3 fusion.40
  173.1 33.7 %all-gather.13.cloned.1.call-done = bf16[1024,1024]{1,0:T(8,128)(2,1)} async-done(((bf16[32,1024]{1,0:T(8,128)(2,1)}), bf16[1024,1024]{1,0:T(8,128)(2,1)}) %all-gather.13.cloned.1.call-update) | async-done | bytes 2097168 | tf_op jit(solution)/shard_map/all_gather | solution.py:128
  206.8 2.4 fusion.94
  213.1 3.6 all-to-all-start
  217.9 2.6 gather_fusion.2
  220.5 28.4 %all-to-all-done = bf16[8,80,1024]{2,1,0:T(8,128)(2,1)S(1)} async-done(((bf16[8,80,1024]{2,1,0:T(8,128)(2,1)}), bf16[8,80,1024]{2,1,0:T(8,128)(2,1)S(1)}, u32[]{:S(2)}, u32[]{:S(2)}) %all-to-all-start) | async-done | bytes 1310752 | tf_op jit(solution)/shard_map/all_to_all | solution.py:179
  248.9 2.8 broadcast_in_dim.41
  251.7 4.6 all-to-all-start.2
  256.3 38.5 %all-gather.15.cloned.1.call-done = bf16[1,2,1024,2048]{3,2,1,0:T(8,128)(2,1)} async-done(((bf16[1,2,1024,512]{3,2,1,0:T(8,128)(2,1)}), bf16[1,2,1024,2048]{3,2,1,0:T(8,128)(2,1)}) %all-gather.15.cloned.1.call-update) | async-done | bytes 8388624 | tf_op jit(solution)/shard_map/all_gather | solution.py:137
  294.8 6.7 fusion.21
  301.5 82.5 %all-gather.17.cloned.1.call-done = bf16[1,2,1024,2048]{3,2,1,0:T(8,128)(2,1)} async-done(((bf16[1,2,1024,512]{3,2,1,0:T(8,128)(2,1)}), bf16[1,2,1024,2048]{3,2,1,0:T(8,128)(2,1)}) %all-gather.17.cloned.1.call-update) | async-done | bytes 8388624 | tf_op jit(solution)/shard_map/all_gather | solution.py:138
  384.0 9.0 fusion.95
  393.0 40.6 %all-gather.2 = bf16[32,32,4]{1,2,0:T(4,128)(2,1)S(1)} all-gather(bf16[1,32,4]{1,2,0:T(4,128)(2,1)S(1)} %bitcast.251), channel_id=1, replica_groups=mesh['rep'=4,'exp'=8] {'rep','exp'}, dimensions={0}, use_global_device_ids=true | all-gather | bytes 8448 | tf_op jit(solution)/shard_map/all_gather | solution.py:131
  436.4 2.1 fusion.62
  438.6 6.0 fusion.25
  444.6 2.3 copy-done.40
  446.9 5.9 fusion.19
  452.8 3.0 fusion.96
  456.2 5.8 fusion.97
  462.3 2.8 collective-permute-done.1
  466.2 5.7 fusion.28
  472.0 9.5 fusion.12
  481.5 7.9 fusion.98
  489.7 3.0 collective-permute-done.3
  493.8 5.4 add_convert_fusion
  500.2 3.5 all-to-all-start.1
  505.7 16.1 %all-to-all-done.1 = bf16[8,40,1024]{2,1,0:T(8,128)(2,1)S(1)} async-done(((bf16[8,40,1024]{2,1,0:T(8,128)(2,1)}), bf16[8,40,1024]{2,1,0:T(8,128)(2,1)S(1)}, u32[]{:S(2)}, u32[]{:S(2)}) %all-to-all-start.1) | async-done | bytes 655392 | tf_op jit(solution)/shard_map/all_to_all | solution.py:184
  521.8 3.5 all-to-all-start.3
  527.4 16.0 %all-to-all-done.3 = bf16[8,40,1024]{2,1,0:T(8,128)(2,1)S(1)} async-done(((bf16[8,40,1024]{2,1,0:T(8,128)(2,1)}), bf16[8,40,1024]{2,1,0:T(8,128)(2,1)S(1)}, u32[]{:S(2)}, u32[]{:S(2)}) %all-to-all-start.3) | async-done | bytes 655392 | tf_op jit(solution)/shard_map/all_to_all | solution.py:227
  545.2 2.3 fusion.58
  550.2 14.8 multiply_reduce_fusion
  567.4 7.7 multiply_convert_fusion
  575.1 3.6 multiply_convert_fusion.3
  579.2 9.6 fusion.32
  590.7 8.5 convert_bitcast_fusion
  599.2 8.3 convert_bitcast_fusion.1
  608.0 6.9 fusion.39
  615.0 35.9 %reduce-scatter.18.cloned.1.call-done = bf16[256,1024]{0,1:T(8,128)(2,1)} async-done(((bf16[1024,1024]{0,1:T(8,128)(2,1)}), bf16[256,1024]{0,1:T(8,128)(2,1)}) %reduce-scatter.18.cloned.1.call-update) | async-done | bytes 524304 | tf_op jit(solution)/shard_map/reduce_scatter | solution.py:270
  650.8 6.3 fusion.54
  659.4 7.4 pad_maximum_fusion.1
  668.2 6.9 convert_bitcast_fusion.2
  675.1 5.0 convert_bitcast_fusion.3
  680.1 7.5 pad_maximum_fusion
  689.0 2.7 fusion.69
  692.7 6.6 fusion.65
  699.3 87.7 %reduce-scatter.32.cloned.1.call-done = f32[32,4]{1,0:T(8,128)} async-done(((f32[1024,4]{1,0:T(8,128)}), f32[32,4]{1,0:T(8,128)}) %reduce-scatter.32.cloned.1.call-update) | async-done | bytes 528
  789.5 130.1 %reduce-scatter.30.cloned.1.call-done = f32[32,2]{1,0:T(8,128)} async-done(((f32[1024,2]{1,0:T(8,128)}), f32[32,2]{1,0:T(8,128)}) %reduce-scatter.30.cloned.1.call-update) | async-done | bytes 272
  921.0 131.1 %reduce-scatter.28.cloned.1.call-done = f32[32,2]{1,0:T(8,128)} async-done(((f32[1024,2]{1,0:T(8,128)}), f32[32,2]{1,0:T(8,128)}) %reduce-scatter.28.cloned.1.call-update) | async-done | bytes 272
  1053.4 84.7 %reduce-scatter.26.cloned.1.call-done = bf16[1,2,1024,512]{3,2,1,0:T(8,128)(2,1)} async-done(((bf16[1,2,1024,2048]{3,2,1,0:T(8,128)(2,1)}), bf16[1,2,1024,512]{3,2,1,0:T(8,128)(2,1)}) %reduce-scatter.26.cloned.1.call-update) | async-done | bytes 2097168 | tf_op jit(solution)/shard_map/reduce_scatter | solution.py:217
  1138.1 4.2 convert_element_type.255
  1142.3 85.1 %reduce-scatter.24.cloned.1.call-done = bf16[1,2,1024,512]{3,2,1,0:T(8,128)(2,1)} async-done(((bf16[1,2,1024,2048]{3,2,1,0:T(8,128)(2,1)}), bf16[1,2,1024,512]{3,2,1,0:T(8,128)(2,1)}) %reduce-scatter.24.cloned.1.call-update) | async-done | bytes 2097168 | tf_op jit(solution)/shard_map/reduce_scatter | solution.py:211
  1227.5 4.2 convert_element_type.253
  1231.7 141.3 %reduce-scatter.22.cloned.1.call-done = f32[32,1024]{1,0:T(8,128)} async-done(((f32[1024,1024]{1,0:T(8,128)}), f32[32,1024]{1,0:T(8,128)}) %reduce-scatter.22.cloned.1.call-update) | async-done | bytes 131088 | tf_op jit(solution)/shard_map/reduce_scatter | solution.py:288
  1373.0 159.9 %reduce-scatter.20.cloned.1.call-done = f32[32,3072]{1,0:T(8,128)} async-done(((f32[1024,3072]{1,0:T(8,128)}), f32[32,3072]{1,0:T(8,128)}) %reduce-scatter.20.cloned.1.call-update) | async-done | bytes 393232 | tf_op jit(solution)/shard_map/reduce_scatter | solution.py:287
  (216 shorter events, 47.1 us)
Async XLA Ops:
  7.2 83.6 %all-gather.9.cloned.1.call-start = ((), (), s32[]{:S(2)}) async-start(), calls=%async_computation.13 | async-start | bytes 6488064 | tf_op jit(solution)/shard_map/all_gather | solution.py:127
  7.9 139.4 %all-gather.11.cloned.1.call-start = ((), (), s32[]{:S(2)}) async-start(), calls=%async_computation.14 | async-start | bytes 5242880 | tf_op jit(solution)/shard_map/all_gather | solution.py:147
  89.3 6.3 copy-start.33
  90.7 5.0 copy-start.35
  90.7 5.0 copy-start.29
  90.7 5.0 copy-start.31
  95.7 3.0 copy-start.37
  95.7 6.4 copy-start.38
  96.8 110.0 %all-gather.13.cloned.1.call-start = ((), (), s32[]{:S(2)}) async-start(), calls=%async_computation.15 | async-start | bytes 2162688 | tf_op jit(solution)/shard_map/all_gather | solution.py:128
  97.5 197.3 %all-gather.15.cloned.1.call-start = ((), (), s32[]{:S(2)}) async-start(), calls=%async_computation.16 | async-start | bytes 10485760 | tf_op jit(solution)/shard_map/all_gather | solution.py:137
  98.1 285.9 %all-gather.17.cloned.1.call-start = ((), (), s32[]{:S(2)}) async-start(), calls=%async_computation.17 | async-start | bytes 10485760 | tf_op jit(solution)/shard_map/all_gather | solution.py:138
  154.8 7.6 copy-start.4
  162.4 6.3 copy-start
  162.4 6.3 copy-start.14
  168.7 38.0 %copy-start.8 = (bf16[1,256,1024]{2,1,0:T(8,128)(2,1)S(1)}, bf16[1,256,1024]{2,1,0:T(8,128)(2,1)}, u32[]{:S(2)}) copy-start(bf16[1,256,1024]{2,1,0:T(8,128)(2,1)} %param.11) | copy-start | bytes 1572868
  173.1 36.4 %copy-start.16 = (bf16[16,64,256]{2,1,0:T(8,128)(2,1)}, bf16[16,64,256]{2,1,0:T(8,128)(2,1)S(1)}, u32[]{:S(2)}) copy-start(bf16[16,64,256]{2,1,0:T(8,128)(2,1)S(1)} %fusion.40) | copy-start | bytes 1572868
  213.1 35.8 %all-to-all-start = ((bf16[8,80,1024]{2,1,0:T(8,128)(2,1)}), bf16[8,80,1024]{2,1,0:T(8,128)(2,1)S(1)}, u32[]{:S(2)}, u32[]{:S(2)}) async-start(bf16[8,80,1024]{2,1,0:T(8,128)(2,1)} %bitcast.216), calls=%async_computation | async-start | bytes 2621440 | tf_op jit(solution)/shard_map/all_to_all | solution.py:179
  248.9 217.4 %copy-start.2 = (bf16[8,80,1024]{2,1,0:T(8,128)(2,1)}, bf16[8,80,1024]{2,1,0:T(8,128)(2,1)S(1)}, u32[]{:S(2)}) copy-start(bf16[8,80,1024]{2,1,0:T(8,128)(2,1)S(1)} %all-to-all-done) | copy-start | bytes 3932164
  251.7 182.6 %all-to-all-start.2 = ((bf16[8,80,1024]{2,1,0:T(8,128)(2,1)}), bf16[8,80,1024]{2,1,0:T(8,128)(2,1)}, u32[]{:S(2)}, u32[]{:S(2)}) async-start(bf16[8,80,1024]{2,1,0:T(8,128)(2,1)} %bitcast.215), calls=%async_computation.2 | async-start | bytes 2621440 | tf_op jit(solution)/shard_map/all_to_all | solution.py:192
  301.5 91.5 %copy-start.39 = (bf16[32,4]{0,1:T(4,128)(2,1)S(1)}, bf16[32,4]{0,1:T(4,128)(2,1)}, u32[]{:S(2)}) copy-start(bf16[32,4]{0,1:T(4,128)(2,1)} %param.18) | copy-start | bytes 772
  393.0 43.0 %collective-permute-start = (bf16[640,1024]{1,0:T(8,128)(2,1)}, bf16[640,1024]{1,0:T(8,128)(2,1)}, u32[]{:S(2)}, u32[]{:S(2)}) collective-permute-start(bf16[640,1024]{1,0:T(8,128)(2,1)} %get-tuple-element.35), channel_id=1, source_target_pairs={{0,1},{1,0},{2,3},{3,2},{4,5},{5,4},{6,7},{7,6},{8,9},{9,8},{10,11... | collective-permute-start | bytes 3932168 | tf_op jit(solution)/shard_map/ppermute | solution.py:16
  436.4 10.5 slice-start.6
  438.6 6.0 copy-start.24
  438.6 8.3 slice-start.7
  438.6 14.2 slice-start.4
  446.9 5.9 slice-start.5
  452.8 3.0 copy-start.41
  455.8 6.5 collective-permute-start.2
  462.0 3.1 collective-permute-start.1
  472.0 9.5 copy-start.11
  481.5 7.9 copy-start.42
  489.5 3.2 collective-permute-start.3
  500.2 21.6 %all-to-all-start.1 = ((bf16[8,40,1024]{2,1,0:T(8,128)(2,1)}), bf16[8,40,1024]{2,1,0:T(8,128)(2,1)S(1)}, u32[]{:S(2)}, u32[]{:S(2)}) async-start(bf16[8,40,1024]{2,1,0:T(8,128)(2,1)} %dynamic-slice_bitcast_fusion.1), calls=%async_computation.1 | async-start | bytes 1310720 | tf_op jit(solution)/shard_map/all_to_all | solution.py:184
  521.8 21.6 %all-to-all-start.3 = ((bf16[8,40,1024]{2,1,0:T(8,128)(2,1)}), bf16[8,40,1024]{2,1,0:T(8,128)(2,1)S(1)}, u32[]{:S(2)}, u32[]{:S(2)}) async-start(bf16[8,40,1024]{2,1,0:T(8,128)(2,1)} %dynamic-slice_bitcast_fusion), calls=%async_computation.3 | async-start | bytes 1310720 | tf_op jit(solution)/shard_map/all_to_all | solution.py:227
  525.4 89.6 %reduce-scatter.16.cloned.1.call-start = ((), (), s32[]{:S(2)}) async-start(), calls=%async_computation.18 | async-start | bytes 2621440 | tf_op jit(solution)/shard_map/reduce_scatter | solution.py:264
  527.4 17.8 %copy-start.18 = (bf16[256,1024]{1,0:T(8,128)(2,1)S(1)}, bf16[256,1024]{1,0:T(8,128)(2,1)}, u32[]{:S(2)}) copy-start(bf16[256,1024]{1,0:T(8,128)(2,1)} %gather_fusion.1) | copy-start | bytes 1572868
  544.6 3.8 copy-start.13
  550.2 14.8 slice-start
  550.2 14.8 slice-start.1
  550.2 16.0 %slice-start.2 = ((s8[16777216]{0:T(1024)(128)(4,1)}), s8[4194304]{0:T(1024)(128)(4,1)S(1)}, s32[]{:S(2)}) async-start(s8[16777216]{0:T(1024)(128)(4,1)} %bitcast.200), calls=%async_computation.29 | async-start | bytes 8388608
  550.2 17.2 %slice-start.3 = ((s8[16777216]{0:T(1024)(128)(4,1)}), s8[4194304]{0:T(1024)(128)(4,1)S(1)}, s32[]{:S(2)}) async-start(s8[16777216]{0:T(1024)(128)(4,1)} %bitcast.200), calls=%async_computation.30 | async-start | bytes 8388608
  575.1 4.0 copy-start.1
  575.1 4.1 copy-start.15
  579.1 10.1 copy-start.3
  579.2 11.5 copy-start.20
  579.2 71.7 %reduce-scatter.18.cloned.1.call-start = ((), (), s32[]{:S(2)}) async-start(), calls=%async_computation.19 | async-start | bytes 2621440 | tf_op jit(solution)/shard_map/reduce_scatter | solution.py:270
  588.8 198.1 %reduce-scatter.32.cloned.1.call-start = ((), (), s32[]{:S(2)}) async-start(), calls=%async_computation.26 | async-start | bytes 540672
  590.7 8.5 copy-start.12
  599.2 8.9 copy-start.5
  607.5 43.4 %copy-start.30 = (f32[1024,1]{0,1:T(1,128)S(1)}, f32[1024,1]{0,1:T(1,128)}, u32[]{:S(2)}) copy-start(f32[1024,1]{0,1:T(1,128)} %copy-done.29) | copy-start | bytes 12292
  607.5 43.3 %copy-start.34 = (f32[256]{0:T(256)S(1)}, f32[256]{0:T(256)}, u32[]{:S(2)}) copy-start(f32[256]{0:T(256)} %copy-done.33) | copy-start | bytes 3076
  607.5 43.3 %copy-start.36 = (f32[256]{0:T(256)S(1)}, f32[256]{0:T(256)}, u32[]{:S(2)}) copy-start(f32[256]{0:T(256)} %copy-done.35) | copy-start | bytes 3076
  607.5 312.1 %reduce-scatter.30.cloned.1.call-start = ((), (), s32[]{:S(2)}) async-start(), calls=%async_computation.25 | async-start | bytes 540672
  658.3 393.8 %reduce-scatter.28.cloned.1.call-start = ((), (), s32[]{:S(2)}) async-start(), calls=%async_computation.24 | async-start | bytes 540672
  659.4 478.8 %reduce-scatter.26.cloned.1.call-start = ((), (), s32[]{:S(2)}) async-start(), calls=%async_computation.23 | async-start | bytes 10485760 | tf_op jit(solution)/shard_map/reduce_scatter | solution.py:217
  666.9 560.6 %reduce-scatter.24.cloned.1.call-start = ((), (), s32[]{:S(2)}) async-start(), calls=%async_computation.22 | async-start | bytes 10485760 | tf_op jit(solution)/shard_map/reduce_scatter | solution.py:211
  668.2 6.9 copy-start.43
  687.6 4.3 copy-start.9
  687.6 4.3 copy-start.19
  687.7 4.3 copy-start.27
  687.7 4.3 copy-start.32
  687.7 685.3 %reduce-scatter.22.cloned.1.call-start = ((), (), s32[]{:S(2)}) async-start(), calls=%async_computation.21 | async-start | bytes 4325376 | tf_op jit(solution)/shard_map/reduce_scatter | solution.py:288
  691.7 841.2 %reduce-scatter.20.cloned.1.call-start = ((), (), s32[]{:S(2)}) async-start(), calls=%async_computation.20 | async-start | bytes 12976128 | tf_op jit(solution)/shard_map/reduce_scatter | solution.py:287
  699.3 89.1 %copy-start.26 = (f32[256,1024]{1,0:T(8,128)S(1)}, f32[256,1024]{1,0:T(8,128)}, u32[]{:S(2)}) copy-start(f32[256,1024]{1,0:T(8,128)} %get-tuple-element.45) | copy-start | bytes 3145732
  (10 other events, 15.4 us)
Sparse Core Ops, SparseCore 0:
  11.0 72.1 all-gather.8
  96.9 50.2 all-gather.10
  150.3 56.4 all-gather.12
  208.5 86.3 all-gather.14
  296.5 87.4 all-gather.16
  579.3 33.0 reduce-scatter.15
  615.6 35.1 reduce-scatter.17
  653.1 133.8 reduce-scatter.31
  789.3 130.2 reduce-scatter.29
  921.7 130.3 reduce-scatter.27
  1055.4 82.6 reduce-scatter.25
  1141.1 86.3 reduce-scatter.23
  1230.4 142.5 reduce-scatter.21
  1380.5 152.3 reduce-scatter.19
where the time goes:
time: 1540 us
  waiting for transfers between devices  1120 us (73%)
  matrix products  149 us (10%)
  blocking collectives  121 us (8%)
  other arithmetic  59.1 us (4%)
  local copies, waits for them, and re-layouts  54.5 us (4%)
  starting transfers between devices  17.6 us (1%)
    unnamed x17, waiting for transfers between devices  351 us
    reduce_scatter x1, waiting for transfers between devices, local(): lax.psum_scatter(grad_qkv, ('rep', 'exp'), scatter_dimension=0, tiled=True)  160 us
    reduce_scatter x1, waiting for transfers between devices, local(): lax.psum_scatter(grad_proj, ('rep', 'exp'), scatter_dimension=0, tiled=True)  141 us
    reduce_scatter x1, waiting for transfers between devices, local(): lax.psum_scatter(jnp.stack([in_early, in_late])[None].astype(jnp.bfloat16...  85.1 us
    reduce_scatter x1, waiting for transfers between devices, local(): lax.psum_scatter(jnp.stack([out_early, out_late])[None].astype(jnp.bfloat...  84.7 us
    all_gather x1, waiting for transfers between devices, local(): lax.all_gather(w_out, 'rep', axis=3, tiled=True)  82.5 us
    all_gather x1, waiting for transfers between devices, local(): lax.all_gather(projected[:, model_width:], 'rep', axis=0, tiled=True)  44.5 us
    all_gather x1, blocking collectives, local(): lax.all_gather(norm_gains, ('rep', 'exp'), axis=0, tiled=True)  43.2 us
  transfers between devices with their start and end apart: 22, of which 17 were waited for; matrix products, arithmetic and copies ran while one was open for 11% of the time, Pallas kernels for 0%

commit v1 on v0

v1 whole, which is shorter than its diff:
```python
import jax
import jax.numpy as jnp
from jax import lax
from jax.sharding import PartitionSpec as P

HEAD_DIM = 64
REPS = 4
eps = 1e-05
neg_fill = -1e30
bf16 = jnp.bfloat16
f32 = jnp.float32


def flip(value, axis, mask):
    pairs = [(source, source ^ mask) for source in range(lax.axis_size(axis))]
    return lax.ppermute(value, axis, pairs)


def over_x(value):
    return flip(value, "rep", 1)


def over_y(value):
    return flip(value, "rep", 2)


def over_diag(value):
    return flip(value, "rep", 3)


def over_core(value):
    return flip(value, "exp", 1)


def shift_z(value, step):
    size = lax.axis_size("exp")
    if step % (size // 2) == 0:
        return value
    pairs = [(source, (source + 2 * step) % size) for source in range(size)]
    return lax.ppermute(value, "exp", pairs)


def gather_plane(first, second):
    first_x, second_y = over_x(first), over_y(second)
    first_y, second_x = over_y(first), over_x(second)
    return (
        [first, first_x, first_y, over_y(first_x)],
        [second, second_x, second_y, over_x(second_y)],
    )


def scatter_plane_x(blocks):
    low = [block.astype(bf16) for block in blocks]
    kept = blocks[0].astype(f32) + over_x(low[1]).astype(f32)
    passed = blocks[2].astype(f32) + over_x(low[3]).astype(f32)
    return kept + over_y(passed.astype(bf16)).astype(f32)


def scatter_plane_y(blocks):
    low = [block.astype(bf16) for block in blocks]
    kept = blocks[0].astype(f32) + over_y(low[2]).astype(f32)
    passed = blocks[1].astype(f32) + over_y(low[3]).astype(f32)
    return kept + over_x(passed.astype(bf16)).astype(f32)


def pick(stacked, index, axis=0):
    return lax.dynamic_index_in_dim(stacked, index, axis=axis, keepdims=False)


def gather_z(block):
    n_z = lax.axis_size("exp") // 2
    own_z = lax.axis_index("exp") // 2
    out = jnp.zeros((n_z,) + block.shape, block.dtype)
    for step in range(n_z):
        out = lax.dynamic_update_index_in_dim(out, shift_z(block, step), (own_z - step) % n_z, 0)
    return out


def scatter_z(blocks):
    n_z = lax.axis_size("exp") // 2
    own_z = lax.axis_index("exp") // 2
    total = pick(blocks, own_z)
    for step in range(1, n_z):
        sent = pick(blocks, (own_z + step) % n_z).astype(bf16)
        total = total + shift_z(sent, step).astype(f32)
    return total


def both_cores(value, parity, axis):
    other = over_core(value)
    return jnp.stack(
        [jnp.where(parity == 0, value, other), jnp.where(parity == 0, other, value)], axis=axis
    )


def layer_norm(values, gain_vec, shift):
    average = jnp.mean(values, axis=-1, keepdims=True)
    centred = values - average
    inverse = lax.rsqrt(jnp.mean(centred * centred, axis=-1, keepdims=True) + eps)
    normed = centred * inverse
    return (normed * gain_vec + shift, normed, inverse)


def norm_back(gradient, normed, inverse, gain_vec):
    scaled = gradient * gain_vec
    bracket = (
        scaled
        - jnp.mean(scaled, axis=-1, keepdims=True)
        - normed * jnp.mean(scaled * normed, axis=-1, keepdims=True)
    )
    return inverse * bracket


def contract_rows(former, latter):
    return lax.dot_general(former, latter, (((0,), (0,)), ((), ())), preferred_element_type=f32)


def contract_last(former, latter):
    return lax.dot_general(former, latter, (((1,), (1,)), ((), ())), preferred_element_type=f32)


def product(former, latter):
    return jnp.dot(former, latter, preferred_element_type=f32)


def local(
    tokens,
    doc_ids,
    routes,
    norm_gains,
    norm_biases,
    w_qkv,
    w_proj,
    centroids,
    w_in,
    w_out,
    grad_out,
):
    rep = lax.axis_index("rep")
    parity = lax.axis_index("exp") % 2
    own_z = lax.axis_index("exp") // 2
    n_z = lax.axis_size("exp") // 2
    tok_rows = tokens.shape[1]
    width = tokens.shape[2]
    experts = centroids.shape[1]
    capacity = 2 * (5 * tok_rows // (8 * experts))
    group = width // REPS
    heads = group // HEAD_DIM
    shard = w_qkv.shape[0]
    score_scale = HEAD_DIM ** (-0.5)

    half = tok_rows // 2
    own_tokens = tokens[0]
    tok_a, tok_b = gather_plane(own_tokens[:half], own_tokens[half:])
    seq = jnp.concatenate([part for pair in zip(tok_a, tok_b) for part in pair], axis=0)

    extra = 4 + experts
    pad = -extra % 128
    small = jnp.concatenate(
        [norm_gains, norm_biases, centroids, jnp.zeros((shard, pad), bf16)], axis=1
    )
    by_rep = w_qkv.reshape(shard, 3, REPS, group)
    sends = [
        jnp.concatenate([pick(by_rep, rep ^ k, 2).reshape(shard, 3 * group), small], axis=1)
        for k in range(REPS)
    ]
    got = jnp.stack([sends[0], over_x(sends[1]), over_y(sends[2]), over_diag(sends[3])])
    got = jnp.stack([pick(got, rep ^ k) for k in range(REPS)])
    along = gather_z(got)
    whole = both_cores(along, parity, 1)
    whole = whole.transpose(2, 0, 1, 3, 4).reshape(width, 3 * group + extra + pad)
    qkv_w = whole[:, : 3 * group]
    params = whole[:, 3 * group : 3 * group + extra].T.astype(f32)
    centroid = pick(whole[:, 3 * group + 4 : 3 * group + extra], own_z, 1)

    expert = routes[0, :, 0]
    onehot = (expert[:, None] == jnp.arange(experts, dtype=jnp.int32)[None, :]).astype(jnp.int32)
    before = jnp.cumsum(onehot, axis=0) - onehot
    rank = jnp.sum(before * onehot, axis=1)
    slot = ((expert - own_z) % n_z) * capacity + rank
    table = (jnp.arange(n_z * capacity, dtype=jnp.int32)[:, None] == slot[None, :]).astype(bf16)

    def dispatch(values):
        packed = product(table, values).astype(bf16).reshape(n_z, capacity, width)
        mine = jnp.concatenate([shift_z(packed[step], step) for step in range(n_z)], axis=0)
        return jnp.concatenate([mine, over_core(mine)], axis=0)

    def recall(rows):
        rows = rows.reshape(n_z, capacity, width)
        back = jnp.concatenate([shift_z(rows[step], -step) for step in range(n_z)], axis=0)
        return contract_rows(table, back)

    own_grad = grad_out[0]
    grad_rows = dispatch(own_grad).astype(f32)

    proj_core = gather_z(w_proj)
    proj_half = n_z // 2
    proj_a, proj_b = gather_plane(proj_core[:proj_half], proj_core[proj_half:])
    proj_w = [
        both_cores(jnp.concatenate(pair, axis=0), parity, 1).reshape(group, width)
        for pair in zip(proj_a, proj_b)
    ]

    layers = [gather_plane(w_in[0, sub], w_out[0, sub]) for sub in range(2)]

    seq32 = seq.astype(f32)
    normed, unit_in, inverse_in = layer_norm(seq32, params[0], params[2])
    attn_in = normed.astype(bf16)
    qkv = product(attn_in, qkv_w).astype(bf16)
    seq_len = qkv.shape[0]
    query, keys, values = [
        qkv[:, part * group : (part + 1) * group].reshape(seq_len, heads, HEAD_DIM)
        for part in range(3)
    ]
    docs = doc_ids[0].reshape(REPS, tok_rows)
    doc_rel = jnp.concatenate([pick(docs, rep ^ k) for k in range(REPS)])
    pos = jnp.concatenate([(rep ^ k) * tok_rows + jnp.arange(tok_rows) for k in range(REPS)])
    allowed = (pos[None, :] <= pos[:, None]) & (doc_rel[None, :] == doc_rel[:, None])
    raw = jnp.einsum("qhd,khd->hqk", query, keys, preferred_element_type=f32) * score_scale
    scores = jnp.where(allowed[None], raw, neg_fill)
    probs = jax.nn.softmax(scores, axis=-1)
    probs_b = probs.astype(bf16)
    mixed = jnp.einsum("hqk,khd->qhd", probs_b, values, preferred_element_type=f32)
    mixed = mixed.astype(bf16).reshape(REPS, tok_rows, group)
    mixed = [mixed[0], over_x(mixed[1]), over_y(mixed[2]), over_diag(mixed[3])]
    tokens32 = own_tokens.astype(f32)
    hidden = tokens32 + sum(product(mixed[k], proj_w[k]) for k in range(REPS))
    normed_mid, unit_mid, inverse_mid = layer_norm(hidden, params[1], params[3])
    expert_inputs = normed_mid.astype(bf16)

    own_slots = n_z * capacity
    rows = dispatch(expert_inputs)

    def swap(partial_sum):
        low = partial_sum.astype(bf16)
        return jnp.concatenate([over_core(low[own_slots:]), over_core(low[:own_slots])], axis=0)

    def own_total(partial_sum):
        sent = partial_sum[own_slots:].astype(bf16)
        return partial_sum[:own_slots] + over_core(sent).astype(f32)

    gating = jax.nn.sigmoid(product(rows, centroid))
    stream = rows.astype(f32)
    stored = []
    for sub in range(2):
        ins, outs = layers[sub]
        stream_b = stream.astype(bf16)
        pre = [product(stream_b, w) for w in ins]
        active = [jax.nn.gelu(u).astype(bf16) for u in pre]
        partial_sum = sum(contract_last(g, w) for g, w in zip(active, outs))
        stored.append((stream_b, pre, active))
        if sub == 0:
            stream = stream + partial_sum + swap(partial_sum).astype(f32)
        else:
            final = stream[:own_slots] + own_total(partial_sum)
    own_gate = gating[:own_slots]
    answer = (own_gate[:, None] * final).astype(bf16)
    combined = recall(answer)
    block_out = (hidden + combined).astype(bf16)

    own_rows32 = rows[:own_slots].astype(f32)
    grad_score = jnp.sum(grad_rows[:own_slots] * final, axis=-1) * own_gate * (1.0 - own_gate)
    grad_centroid = jnp.sum(grad_score[:, None] * own_rows32, axis=0)
    grad_stream = gating[:, None] * grad_rows
    grads_in, grads_out = [None, None], [None, None]
    for sub in (1, 0):
        ins, outs = layers[sub]
        stream_b, pre, active = stored[sub]
        branch = grad_stream.astype(bf16)
        grad_pre = []
        for u, w in zip(pre, outs):
            unused, gelu_back = jax.vjp(jax.nn.gelu, u)
            grad_pre.append(gelu_back(product(branch, w))[0].astype(bf16))
        partial_sum = sum(contract_last(du, w) for du, w in zip(grad_pre, ins))
        grads_in[sub] = scatter_plane_x([contract_rows(stream_b, du) for du in grad_pre])
        grads_out[sub] = scatter_plane_y([contract_rows(branch, g) for g in active])
        if sub == 1:
            grad_stream = grad_stream + partial_sum + swap(partial_sum).astype(f32)
        else:
            grad_first_rows = grad_stream[:own_slots] + own_total(partial_sum)
    grad_w_in = jnp.stack(grads_in)[None]
    grad_w_out = jnp.stack(grads_out)[None]
    grad_inputs = grad_first_rows + grad_score[:, None] * centroid.astype(f32)
    grad_mid = recall(grad_inputs.astype(bf16))

    grad_gain_mid = jnp.sum(grad_mid * unit_mid, axis=0)
    grad_bias_mid = jnp.sum(grad_mid, axis=0)
    grad_hidden = own_grad.astype(f32) + norm_back(grad_mid, unit_mid, inverse_mid, params[1])
    grad_hidden_b = grad_hidden.astype(bf16)
    grad_mixed = [contract_last(grad_hidden_b, w).astype(bf16) for w in proj_w]
    grad_mixed = [
        grad_mixed[0],
        over_x(grad_mixed[1]),
        over_y(grad_mixed[2]),
        over_diag(grad_mixed[3]),
    ]
    grad_mixed = jnp.concatenate(grad_mixed, axis=0).reshape(seq_len, heads, HEAD_DIM)

    def own_parity(blocks):
        axis = blocks.ndim - 3
        sent = pick(blocks, 1 - parity, axis).astype(bf16)
        return pick(blocks, parity, axis) + over_core(sent).astype(f32)

    proj_parts = [
        own_parity(contract_rows(o, grad_hidden_b).reshape(n_z, 2, shard, width)) for o in mixed
    ]
    proj_plane = jnp.concatenate(
        [
            scatter_plane_x([part[:proj_half] for part in proj_parts]),
            scatter_plane_y([part[proj_half:] for part in proj_parts]),
        ],
        axis=0,
    )
    grad_proj = scatter_z(proj_plane)

    grad_values = jnp.einsum("hqk,qhd->khd", probs_b, grad_mixed, preferred_element_type=f32)
    grad_probs = jnp.einsum("qhd,khd->hqk", grad_mixed, values, preferred_element_type=f32)
    grad_scores = (
        probs * (grad_probs - jnp.sum(grad_probs * probs, axis=-1, keepdims=True))
    ).astype(bf16)
    grad_query = score_scale * jnp.einsum(
        "hqk,khd->qhd", grad_scores, keys, preferred_element_type=f32
    )
    grad_keys = score_scale * jnp.einsum(
        "hqk,qhd->khd", grad_scores, query, preferred_element_type=f32
    )
    grad_qkv_b = jnp.concatenate(
        [g.reshape(seq_len, group).astype(bf16) for g in (grad_query, grad_keys, grad_values)],
        axis=1,
    )
    grad_attn = contract_last(grad_qkv_b, qkv_w)
    blocks = grad_attn.reshape(REPS, 2, half, width)
    grad_attn_own = jnp.concatenate(
        [
            scatter_plane_x([blocks[k, 0] for k in range(REPS)]),
            scatter_plane_y([blocks[k, 1] for k in range(REPS)]),
        ],
        axis=0,
    )
    grad_first = norm_back(grad_attn_own, unit_in[:tok_rows], inverse_in[:tok_rows], params[0])
    grad_tokens = (grad_hidden + grad_first).astype(bf16)

    column_mask = (jnp.arange(experts) == own_z).astype(f32)
    small_grads = jnp.concatenate(
        [
            jnp.stack(
                [
                    jnp.sum(grad_attn * unit_in, axis=0),
                    grad_gain_mid,
                    jnp.sum(grad_attn, axis=0),
                    grad_bias_mid,
                ],
                axis=1,
            ),
            grad_centroid[:, None] * column_mask[None, :],
            jnp.zeros((width, pad), f32),
        ],
        axis=1,
    )
    qkv_part = jnp.concatenate([contract_rows(attn_in, grad_qkv_b), small_grads], axis=1)
    columns = qkv_part.shape[1]
    qkv_part = own_parity(qkv_part.reshape(REPS, n_z, 2, shard, columns))
    qkv_part = scatter_z(qkv_part.transpose(1, 0, 2, 3)).astype(bf16)
    sends = [pick(qkv_part, rep ^ k) for k in range(REPS)]
    got = jnp.stack([sends[0], over_x(sends[1]), over_y(sends[2]), over_diag(sends[3])])
    got = got.astype(f32)
    small_sum = jnp.sum(got[:, :, 3 * group : 3 * group + extra], axis=0)
    big = jnp.stack([pick(got, rep ^ k) for k in range(REPS)])[:, :, : 3 * group]
    grad_qkv = big.reshape(REPS, shard, 3, group).transpose(1, 2, 0, 3).reshape(shard, 3 * width)
    return (
        block_out[None],
        grad_tokens[None],
        small_sum[:, 0:2],
        small_sum[:, 2:4],
        grad_qkv,
        grad_proj,
        small_sum[:, 4:],
        grad_w_in,
        grad_w_out,
    )


def solution(mesh):
    in_specs = (
        P("exp", "rep", None),
        P("exp", None),
        P("exp", "rep", None),
        P(("rep", "exp"), None),
        P(("rep", "exp"), None),
        P(("rep", "exp"), None),
        P(("rep", "exp"), None),
        P(("rep", "exp"), None),
        P("exp", None, None, "rep"),
        P("exp", None, None, "rep"),
        P("exp", "rep", None),
    )
    out_specs = (
        P("exp", "rep", None),
        P("exp", "rep", None),
        P(("rep", "exp"), None),
        P(("rep", "exp"), None),
        P(("rep", "exp"), None),
        P(("rep", "exp"), None),
        P(("rep", "exp"), None),
        P("exp", None, None, "rep"),
        P("exp", None, None, "rep"),
    )
    return jax.shard_map(local, mesh=mesh, in_specs=in_specs, out_specs=out_specs, check_vma=False)
```

time: 1540 us -> 639 us (0.41)
  waiting for transfers between devices: 1120 us -> 278 us
  blocking collectives: 121 us -> 0 us
  starting transfers between devices: 17.6 us -> 112 us
  other arithmetic: 59.1 us -> 39.9 us
    reduce_scatter x6 -> x0, waiting for transfers between devices: 507 us -> none  [the longest x1 160 us: local(): lax.psum_scatter(grad_qkv, ('rep', 'exp'), scatter_dimension=0, tiled=True)]
    unnamed x17 -> x0, waiting for transfers between devices: 351 us -> none
    ppermute x4 -> x102, waiting for transfers between devices: 5.83 us -> 278 us  [the longest x78 221 us: flip(): return lax.ppermute(value, axis, pairs)]
    all_gather x5 -> x0, waiting for transfers between devices: 199 us -> none  [the longest x1 82.5 us: local(): lax.all_gather(w_out, 'rep', axis=3, tiled=True)]
    all_gather x3 -> x0, blocking collectives: 121 us -> none  [the longest x1 43.2 us: local(): lax.all_gather(norm_gains, ('rep', 'exp'), axis=0, tiled=True)]
    ppermute x4 -> x102, starting transfers between devices: 0.84 us -> 112 us  [the longest x78 65.9 us: flip(): return lax.ppermute(value, axis, pairs)]
    all_to_all x4 -> x0, waiting for transfers between devices: 60.5 us -> none  [the longest x1 28.4 us: local(): lax.all_to_all(send_rows, 'exp', split_axis=0, concat_axis=0, tiled=True)]
    dot_general x13 -> x29, matrix products: 78 us -> 57.3 us  [the longest x24 26 us: product(): return jnp.dot(former, latter, preferred_element_type=f32)]
  transfers between devices with their start and end apart: 22 -> 102, of which waited for: 17 -> 37; matrix products, arithmetic and copies ran while one was open for 11% -> 34% of each run, Pallas kernels for 0% -> 0%
where the time goes in v1:
time: 639 us; the launch traced here: 629 us
  waiting for transfers between devices  278 us (44%)
  matrix products  137 us (21%)
  starting transfers between devices  112 us (18%)
  local copies, waits for them, and re-layouts  58.6 us (9%)
  other arithmetic  39.9 us (6%)
    ppermute x78, waiting for transfers between devices, flip(): return lax.ppermute(value, axis, pairs)  221 us
    ppermute x78, starting transfers between devices, flip(): return lax.ppermute(value, axis, pairs)  65.9 us
    ppermute x24, waiting for transfers between devices, shift_z(): return lax.ppermute(value, 'exp', pairs)  56.4 us
    ppermute x24, starting transfers between devices, shift_z(): return lax.ppermute(value, 'exp', pairs)  46.3 us
    dot_general x23, matrix products, contract_rows(): lax.dot_general(former, latter, (((0,), (0,)), ((), ())), preferred_eleme...  44.1 us
    dot_general x24, matrix products, product(): return jnp.dot(former, latter, preferred_element_type=f32)  26 us
    dot_general x21, matrix products, contract_last(): lax.dot_general(former, latter, (((1,), (1,)), ((), ())), preferred_eleme...  25.4 us
    unnamed x259, local copies, waits for them, and re-layouts  18.5 us
  transfers between devices with their start and end apart: 102, of which 37 were waited for; matrix products, arithmetic and copies ran while one was open for 34% of the time, Pallas kernels for 0%

profile of v1, /device:TPU:0, one launch (start us, length us, event | category | flops | bytes accessed | tf_op | source)
XLA Modules:
  0.0 628.8 jit_solution(16192905608734249908)
XLA Ops:
  0.7 3.1 collective-permute-start.13
  3.7 2.6 collective-permute-start.14
  19.7 3.1 slice_bitcast_fusion.1
  37.2 2.7 collective-permute-done.22
  40.8 2.6 collective-permute-done.18
  48.5 2.3 collective-permute-start.33
  51.7 3.6 collective-permute-start.10
  55.6 8.6 %collective-permute-done.9 = bf16[4,32,896]{2,1,0:T(8,128)(2,1)S(1)} collective-permute-done((bf16[4,32,896]{2,1,0:T(8,128)(2,1)S(1)}, bf16[4,32,896]{2,1,0:T(8,128)(2,1)S(1)}, u32[]{:S(2)}, u32[]{:S(2)}) %collective-permute-start.9) | collective-permute-done | bytes 229408 | tf_op jit(solution)/shard_map/ppermute | solution.py:40
  64.3 4.9 collective-permute-done.10
  71.2 4.0 collective-permute-done.26
  79.0 5.0 collective-permute-done.4
  90.9 2.2 convolution_convert_fusion
  94.5 10.2 %fusion.207 = (f32[4,1024]{1,0:T(4,128)S(1)}, f32[4,1024,1024]{1,2,0:T(8,128)}) fusion(pred[1024,1024]{0,1:T(8,128)(4,1)S(1)} %copy-done.46, bf16[1024,4,64]{0,2,1:T(8,128)(2,1)S(1)} %bitcast.410, bf16[1024,4,64]{0,2,1:T(8,128)(2,1)S(1)} %bitcast.412), kind=kOutput, calls=%fused_computation.439 | convolution fusion | flops 553649152 | bytes 18890752 | tf_op jit(solution)/shard_map/sub | solution.py:221
  104.7 7.5 %fusion.89 = bf16[1024,4,64]{0,2,1:T(8,128)(2,1)S(1)} fusion(bf16[1024,4,64]{0,2,1:T(8,128)(2,1)} %bitcast.422, f32[4,1024,1024]{1,2,0:T(8,128)} %get-tuple-element.127, f32[4,1024]{1,0:T(4,128)S(1)} %get-tuple-element.126), kind=kOutput, calls=%fused_computation.162 | convolution fusion | flops 545521664 | bytes 17842176 | tf_op jit(solution)/shard_map/hqk,khd->qhd/dot_general | solution.py:223
  116.2 2.5 collective-permute-done.17
  123.9 4.8 collective-permute-start.29
  128.9 2.3 collective-permute-start.31
  133.4 10.7 %collective-permute-start.52 = (bf16[80,1024]{1,0:T(8,128)(2,1)}, bf16[80,1024]{1,0:T(8,128)(2,1)}, u32[]{:S(2)}, u32[]{:S(2)}) collective-permute-start(bf16[80,1024]{1,0:T(8,128)(2,1)} %get-tuple-element.72), channel_id=1, source_target_pairs={{0,4},{1,5},{2,6},{3,7},{4,0},{5,1},{6,2},{7,3},{8,12},{9,13},{10,... | collective-permute-start | bytes 491528 | tf_op jit(solution)/shard_map/ppermute | solution.py:40
  144.1 4.8 collective-permute-start.53
  160.2 2.6 fusion.213
  162.8 13.3 %collective-permute-done.35 = bf16[1024,512]{1,0:T(8,128)(2,1)S(1)} collective-permute-done((bf16[1024,512]{1,0:T(8,128)(2,1)}, bf16[1024,512]{1,0:T(8,128)(2,1)S(1)}, u32[]{:S(2)}, u32[]{:S(2)}) %collective-permute-start.35) | collective-permute-done | bytes 1048608 | tf_op jit(solution)/shard_map/ppermute | solution.py:16
  178.2 20.4 %collective-permute-done.36 = bf16[1024,512]{1,0:T(8,128)(2,1)S(1)} collective-permute-done((bf16[1024,512]{1,0:T(8,128)(2,1)}, bf16[1024,512]{1,0:T(8,128)(2,1)S(1)}, u32[]{:S(2)}, u32[]{:S(2)}) %collective-permute-start.36) | collective-permute-done | bytes 1048608 | tf_op jit(solution)/shard_map/ppermute | solution.py:16
  198.5 22.5 %collective-permute-done.37 = bf16[1024,512]{1,0:T(8,128)(2,1)S(1)} collective-permute-done((bf16[1024,512]{1,0:T(8,128)(2,1)}, bf16[1024,512]{1,0:T(8,128)(2,1)S(1)}, u32[]{:S(2)}, u32[]{:S(2)}) %collective-permute-start.37) | collective-permute-done | bytes 1048608 | tf_op jit(solution)/shard_map/ppermute | solution.py:16
  225.8 19.5 %collective-permute-done.38 = bf16[1024,512]{1,0:T(8,128)(2,1)S(1)} collective-permute-done((bf16[1024,512]{1,0:T(8,128)(2,1)S(1)}, bf16[1024,512]{1,0:T(8,128)(2,1)S(1)}, u32[]{:S(2)}, u32[]{:S(2)}) %collective-permute-start.38) | collective-permute-done | bytes 1048608 | tf_op jit(solution)/shard_map/ppermute | solution.py:16
  258.6 41.1 %collective-permute-done.45 = bf16[1024,512]{1,0:T(8,128)(2,1)S(1)} collective-permute-done((bf16[1024,512]{1,0:T(8,128)(2,1)S(1)}, bf16[1024,512]{1,0:T(8,128)(2,1)S(1)}, u32[]{:S(2)}, u32[]{:S(2)}) %collective-permute-start.45) | collective-permute-done | bytes 1048608 | tf_op jit(solution)/shard_map/ppermute | solution.py:16
  305.9 2.4 fusion.227
  312.6 2.6 fusion.184
  315.2 2.2 convolution_convert_fusion.1
  321.5 2.1 fusion.220
  327.6 2.7 fusion.185
  334.6 2.2 convolution_convert_fusion.2
  337.5 2.1 convolution_convert_fusion.3
  339.6 2.1 convolution_convert_fusion.4
  341.7 2.5 fusion.180
  351.4 2.2 fusion.221
  354.5 2.4 fusion.226
  366.9 6.1 collective-permute-done.49
  374.9 3.3 add_convert_fusion.3
  378.2 3.6 add_convert_fusion.1
  383.5 2.3 collective-permute-start.59
  389.0 12.0 %collective-permute-done.59 = bf16[80,1024]{1,0:T(8,128)(2,1)S(1)} collective-permute-done((bf16[80,1024]{1,0:T(8,128)(2,1)S(1)}, bf16[80,1024]{1,0:T(8,128)(2,1)S(1)}, u32[]{:S(2)}, u32[]{:S(2)}) %collective-permute-start.59) | collective-permute-done | bytes 163872 | tf_op jit(solution)/shard_map/ppermute | solution.py:40
  417.2 15.5 %multiply_reduce_fusion = (f32[4,1024]{1,0:T(4,128)S(1)}, f32[4,1024,1024]{1,2,0:T(8,128)}) fusion(f32[4,1024,1024]{1,2,0:T(8,128)} %get-tuple-element.127, f32[4,1024]{1,0:T(4,128)S(1)} %get-tuple-element.126, bf16[1024,4,64]{0,2,1:T(8,128)(2,1)S(1)} %bitcast.420, bf16[1024,4,64]{0,2,1:T(8,128)(2,1)S(1)} %bitcast.423), kind=kOutput, calls=%fused_computation.2 | convolution fusion | flops 549449728 | bytes 34635776 | tf_op jit(solution)/shard_map/qhd,khd->hqk/dot_general | solution.py:317
  433.7 7.9 %multiply_convert_fusion = bf16[4,1024,1024]{1,2,0:T(8,128)(2,1)S(1)} fusion(f32[4,1024,1024]{1,2,0:T(8,128)} %get-tuple-element.136, f32[4,1024]{1,0:T(4,128)S(1)} %get-tuple-element.135, f32[4,1024,1024]{1,2,0:T(8,128)S(1)} %bitcast.385, f32[4,1024]{1,0:T(4,128)S(1)} %get-tuple-element.126), kind=kLoop, calls=%fused_computation.1 | loop fusion | flops 16777216 | bytes 41975808 | tf_op jit(solution)/shard_map/convert_element_type | solution.py:320
  443.3 2.7 fusion.88
  446.0 4.0 fusion.83
  450.1 2.4 fusion.109
  454.7 4.6 fusion.192
  461.7 3.9 convert.26
  466.4 6.3 concatenate.114
  476.4 2.4 add_convert_fusion.2
  486.7 3.7 collective-permute-done.85
  499.5 2.4 add_convert_fusion.4
  501.9 22.2 %collective-permute-done.65 = bf16[128,1024]{1,0:T(8,128)(2,1)S(1)} collective-permute-done((bf16[128,1024]{1,0:T(8,128)(2,1)S(1)}, bf16[128,1024]{1,0:T(8,128)(2,1)S(1)}, u32[]{:S(2)}, u32[]{:S(2)}) %collective-permute-start.65) | collective-permute-done | bytes 262176 | tf_op jit(solution)/shard_map/ppermute | solution.py:16
  526.0 4.2 collective-permute-done.89
  534.4 18.8 %collective-permute-done.64 = bf16[128,1024]{1,0:T(8,128)(2,1)S(1)} collective-permute-done((bf16[128,1024]{1,0:T(8,128)(2,1)S(1)}, bf16[128,1024]{1,0:T(8,128)(2,1)S(1)}, u32[]{:S(2)}, u32[]{:S(2)}) %collective-permute-start.64) | collective-permute-done | bytes 262176 | tf_op jit(solution)/shard_map/ppermute | solution.py:16
  553.7 3.1 collective-permute-done.68
  557.9 4.6 collective-permute-done.66
  565.0 22.6 %collective-permute-done.67 = bf16[128,1024]{1,0:T(8,128)(2,1)S(1)} collective-permute-done((bf16[128,1024]{1,0:T(8,128)(2,1)S(1)}, bf16[128,1024]{1,0:T(8,128)(2,1)S(1)}, u32[]{:S(2)}, u32[]{:S(2)}) %collective-permute-start.67) | collective-permute-done | bytes 262176 | tf_op jit(solution)/shard_map/ppermute | solution.py:16
  592.7 7.3 %collective-permute-done.71 = bf16[4,32,896]{2,1,0:T(8,128)(2,1)S(1)} collective-permute-done((bf16[4,32,896]{2,1,0:T(8,128)(2,1)S(1)}, bf16[4,32,896]{2,1,0:T(8,128)(2,1)S(1)}, u32[]{:S(2)}, u32[]{:S(2)}) %collective-permute-start.71) | collective-permute-done | bytes 229408 | tf_op jit(solution)/shard_map/ppermute | solution.py:40
  600.1 6.8 %collective-permute-done.72 = bf16[4,32,896]{2,1,0:T(8,128)(2,1)S(1)} collective-permute-done((bf16[4,32,896]{2,1,0:T(8,128)(2,1)S(1)}, bf16[4,32,896]{2,1,0:T(8,128)(2,1)S(1)}, u32[]{:S(2)}, u32[]{:S(2)}) %collective-permute-start.72) | collective-permute-done | bytes 229408 | tf_op jit(solution)/shard_map/ppermute | solution.py:40
  609.1 4.0 collective-permute-done.73
  614.2 2.6 collective-permute-start.76
  617.4 2.5 maximum_bitcast_fusion.1
  622.3 2.5 maximum_bitcast_fusion
  (637 shorter events, 208.7 us)
Async XLA Ops:
  0.7 31.9 %collective-permute-start.13 = (bf16[32,1024]{1,0:T(8,128)(2,1)}, bf16[32,1024]{1,0:T(8,128)(2,1)}, u32[]{:S(2)}, u32[]{:S(2)}) collective-permute-start(bf16[32,1024]{1,0:T(8,128)(2,1)} %param.17), channel_id=1, source_target_pairs={{0,2},{1,3},{2,4},{3,5},{4,6},{5,7},{6,0},{7,1},{8,10},{9,11},{10,... | collective-permute-start | bytes 196616 | tf_op jit(solution)/shard_map/ppermute | solution.py:40
  3.7 30.3 %collective-permute-start.14 = (bf16[32,1024]{1,0:T(8,128)(2,1)}, bf16[32,1024]{1,0:T(8,128)(2,1)}, u32[]{:S(2)}, u32[]{:S(2)}) collective-permute-start(bf16[32,1024]{1,0:T(8,128)(2,1)} %param.17), channel_id=1, source_target_pairs={{0,4},{1,5},{2,6},{3,7},{4,0},{5,1},{6,2},{7,3},{8,12},{9,13},{10,... | collective-permute-start | bytes 196616 | tf_op jit(solution)/shard_map/ppermute | solution.py:40
  11.7 15.4 %collective-permute-start.6 = (bf16[32,896]{1,0:T(8,128)(2,1)}, bf16[32,896]{1,0:T(8,128)(2,1)}, u32[]{:S(2)}, u32[]{:S(2)}) collective-permute-start(bf16[32,896]{1,0:T(8,128)(2,1)} %concatenate.90), channel_id=1, source_target_pairs={{0,8},{8,0},{16,24},{24,16},{1,9},{9,1},{17,25},{25,17},{2,10},{10... | collective-permute-start | bytes 172040 | tf_op jit(solution)/shard_map/ppermute | solution.py:16
  13.9 14.6 %collective-permute-start.7 = (bf16[32,896]{1,0:T(8,128)(2,1)}, bf16[32,896]{1,0:T(8,128)(2,1)}, u32[]{:S(2)}, u32[]{:S(2)}) collective-permute-start(bf16[32,896]{1,0:T(8,128)(2,1)} %concatenate.91), channel_id=1, source_target_pairs={{0,16},{8,24},{16,0},{24,8},{1,17},{9,25},{17,1},{25,9},{2,18},{10... | collective-permute-start | bytes 172040 | tf_op jit(solution)/shard_map/ppermute | solution.py:16
  16.2 13.9 %collective-permute-start.8 = (bf16[32,896]{1,0:T(8,128)(2,1)}, bf16[32,896]{1,0:T(8,128)(2,1)}, u32[]{:S(2)}, u32[]{:S(2)}) collective-permute-start(bf16[32,896]{1,0:T(8,128)(2,1)} %concatenate.92), channel_id=1, source_target_pairs={{0,24},{8,16},{16,8},{24,0},{1,25},{9,17},{17,9},{25,1},{2,26},{10... | collective-permute-start | bytes 172040 | tf_op jit(solution)/shard_map/ppermute | solution.py:16
  28.6 22.2 %collective-permute-start = (bf16[128,1024]{1,0:T(8,128)(2,1)S(1)}, bf16[128,1024]{1,0:T(8,128)(2,1)S(1)}, u32[]{:S(2)}, u32[]{:S(2)}) collective-permute-start(bf16[128,1024]{1,0:T(8,128)(2,1)S(1)} %get-tuple-element.101), channel_id=1, source_target_pairs={{0,8},{8,0},{16,24},{24,16},{1,9},{9,1},{17,25},{25,17},{2,10},{10... | collective-permute-start | bytes 786440 | tf_op jit(solution)/shard_map/ppermute | solution.py:16
  30.1 21.7 %collective-permute-start.2 = (bf16[128,1024]{1,0:T(8,128)(2,1)S(1)}, bf16[128,1024]{1,0:T(8,128)(2,1)S(1)}, u32[]{:S(2)}, u32[]{:S(2)}) collective-permute-start(bf16[128,1024]{1,0:T(8,128)(2,1)S(1)} %get-tuple-element.101), channel_id=1, source_target_pairs={{0,16},{8,24},{16,0},{24,8},{1,17},{9,25},{17,1},{25,9},{2,18},{10... | collective-permute-start | bytes 786440 | tf_op jit(solution)/shard_map/ppermute | solution.py:16
  32.5 19.0 %collective-permute-start.1 = (bf16[128,1024]{1,0:T(8,128)(2,1)S(1)}, bf16[128,1024]{1,0:T(8,128)(2,1)S(1)}, u32[]{:S(2)}, u32[]{:S(2)}) collective-permute-start(bf16[128,1024]{1,0:T(8,128)(2,1)S(1)} %get-tuple-element.100), channel_id=1, source_target_pairs={{0,8},{8,0},{16,24},{24,16},{1,9},{9,1},{17,25},{25,17},{2,10},{10... | collective-permute-start | bytes 786440 | tf_op jit(solution)/shard_map/ppermute | solution.py:16
  48.5 107.4 %collective-permute-start.33 = (bf16[1024,512]{1,0:T(8,128)(2,1)}, bf16[1024,512]{1,0:T(8,128)(2,1)}, u32[]{:S(2)}, u32[]{:S(2)}) collective-permute-start(bf16[1024,512]{1,0:T(8,128)(2,1)} %get-tuple-element.50), channel_id=1, source_target_pairs={{0,8},{8,0},{16,24},{24,16},{1,9},{9,1},{17,25},{25,17},{2,10},{10... | collective-permute-start | bytes 3145736 | tf_op jit(solution)/shard_map/ppermute | solution.py:16
  50.7 99.1 %collective-permute-start.51 = (bf16[80,1024]{1,0:T(8,128)(2,1)}, bf16[80,1024]{1,0:T(8,128)(2,1)}, u32[]{:S(2)}, u32[]{:S(2)}) collective-permute-start(bf16[80,1024]{1,0:T(8,128)(2,1)} %get-tuple-element.73), channel_id=1, source_target_pairs={{0,2},{1,3},{2,4},{3,5},{4,6},{5,7},{6,0},{7,1},{8,10},{9,11},{10,... | collective-permute-start | bytes 491528 | tf_op jit(solution)/shard_map/ppermute | solution.py:40
  51.5 12.7 %collective-permute-start.9 = (bf16[4,32,896]{2,1,0:T(8,128)(2,1)S(1)}, bf16[4,32,896]{2,1,0:T(8,128)(2,1)S(1)}, u32[]{:S(2)}, u32[]{:S(2)}) collective-permute-start(bf16[4,32,896]{2,1,0:T(8,128)(2,1)S(1)} %pad_maximum_fusion.15), channel_id=1, source_target_pairs={{0,2},{1,3},{2,4},{3,5},{4,6},{5,7},{6,0},{7,1},{8,10},{9,11},{10,... | collective-permute-start | bytes 688136 | tf_op jit(solution)/shard_map/ppermute | solution.py:40
  51.7 17.5 %collective-permute-start.10 = (bf16[4,32,896]{2,1,0:T(8,128)(2,1)S(1)}, bf16[4,32,896]{2,1,0:T(8,128)(2,1)S(1)}, u32[]{:S(2)}, u32[]{:S(2)}) collective-permute-start(bf16[4,32,896]{2,1,0:T(8,128)(2,1)S(1)} %pad_maximum_fusion.15), channel_id=1, source_target_pairs={{0,4},{1,5},{2,6},{3,7},{4,0},{5,1},{6,2},{7,3},{8,12},{9,13},{10,... | collective-permute-start | bytes 688136 | tf_op jit(solution)/shard_map/ppermute | solution.py:40
  55.4 13.8 %collective-permute-start.11 = (bf16[4,32,896]{2,1,0:T(8,128)(2,1)S(1)}, bf16[4,32,896]{2,1,0:T(8,128)(2,1)S(1)}, u32[]{:S(2)}, u32[]{:S(2)}) collective-permute-start(bf16[4,32,896]{2,1,0:T(8,128)(2,1)S(1)} %pad_maximum_fusion.15), channel_id=1, source_target_pairs={{0,6},{1,7},{2,0},{3,1},{4,2},{5,3},{6,4},{7,5},{8,14},{9,15},{10,... | collective-permute-start | bytes 688136 | tf_op jit(solution)/shard_map/ppermute | solution.py:40
  75.2 11.7 %collective-permute-start.20 = (bf16[4,32,1024]{2,1,0:T(8,128)(2,1)S(1)}, bf16[4,32,1024]{2,1,0:T(8,128)(2,1)S(1)}, u32[]{:S(2)}, u32[]{:S(2)}) collective-permute-start(bf16[4,32,1024]{2,1,0:T(8,128)(2,1)S(1)} %constant_dynamic-update-slice_fusion.8), channel_id=1, source_target_pairs={{0,1},{1,0},{2,3},{3,2},{4,5},{5,4},{6,7},{7,6},{8,9},{9,8},{10,11... | collective-permute-start | bytes 786440 | tf_op jit(solution)/shard_map/ppermute | solution.py:16
  128.8 15.4 %collective-permute-start.30 = (bf16[80,1024]{1,0:T(8,128)(2,1)S(1)}, bf16[80,1024]{1,0:T(8,128)(2,1)S(1)}, u32[]{:S(2)}, u32[]{:S(2)}) collective-permute-start(bf16[80,1024]{1,0:T(8,128)(2,1)S(1)} %get-tuple-element.81), channel_id=1, source_target_pairs={{0,4},{1,5},{2,6},{3,7},{4,0},{5,1},{6,2},{7,3},{8,12},{9,13},{10,... | collective-permute-start | bytes 491528 | tf_op jit(solution)/shard_map/ppermute | solution.py:40
  128.9 20.0 %collective-permute-start.31 = (bf16[80,1024]{1,0:T(8,128)(2,1)S(1)}, bf16[80,1024]{1,0:T(8,128)(2,1)S(1)}, u32[]{:S(2)}, u32[]{:S(2)}) collective-permute-start(bf16[80,1024]{1,0:T(8,128)(2,1)S(1)} %get-tuple-element.80), channel_id=1, source_target_pairs={{0,6},{1,7},{2,0},{3,1},{4,2},{5,3},{6,4},{7,5},{8,14},{9,15},{10,... | collective-permute-start | bytes 491528 | tf_op jit(solution)/shard_map/ppermute | solution.py:40
  133.4 19.4 %collective-permute-start.52 = (bf16[80,1024]{1,0:T(8,128)(2,1)}, bf16[80,1024]{1,0:T(8,128)(2,1)}, u32[]{:S(2)}, u32[]{:S(2)}) collective-permute-start(bf16[80,1024]{1,0:T(8,128)(2,1)} %get-tuple-element.72), channel_id=1, source_target_pairs={{0,4},{1,5},{2,6},{3,7},{4,0},{5,1},{6,2},{7,3},{8,12},{9,13},{10,... | collective-permute-start | bytes 491528 | tf_op jit(solution)/shard_map/ppermute | solution.py:40
  149.8 26.2 %collective-permute-start.35 = (bf16[1024,512]{1,0:T(8,128)(2,1)}, bf16[1024,512]{1,0:T(8,128)(2,1)S(1)}, u32[]{:S(2)}, u32[]{:S(2)}) collective-permute-start(bf16[1024,512]{1,0:T(8,128)(2,1)} %get-tuple-element.50), channel_id=1, source_target_pairs={{0,16},{8,24},{16,0},{24,8},{1,17},{9,25},{17,1},{25,9},{2,18},{10... | collective-permute-start | bytes 3145736 | tf_op jit(solution)/shard_map/ppermute | solution.py:16
  152.8 72.0 %collective-permute-start.34 = (bf16[1024,512]{1,0:T(8,128)(2,1)}, bf16[1024,512]{1,0:T(8,128)(2,1)S(1)}, u32[]{:S(2)}, u32[]{:S(2)}) collective-permute-start(bf16[1024,512]{1,0:T(8,128)(2,1)} %get-tuple-element.51), channel_id=1, source_target_pairs={{0,8},{8,0},{16,24},{24,16},{1,9},{9,1},{17,25},{25,17},{2,10},{10... | collective-permute-start | bytes 3145736 | tf_op jit(solution)/shard_map/ppermute | solution.py:16
  153.3 45.2 %collective-permute-start.36 = (bf16[1024,512]{1,0:T(8,128)(2,1)}, bf16[1024,512]{1,0:T(8,128)(2,1)S(1)}, u32[]{:S(2)}, u32[]{:S(2)}) collective-permute-start(bf16[1024,512]{1,0:T(8,128)(2,1)} %get-tuple-element.51), channel_id=1, source_target_pairs={{0,16},{8,24},{16,0},{24,8},{1,17},{9,25},{17,1},{25,9},{2,18},{10... | collective-permute-start | bytes 3145736 | tf_op jit(solution)/shard_map/ppermute | solution.py:16
  155.8 97.0 %collective-permute-start.41 = (bf16[1024,512]{1,0:T(8,128)(2,1)S(1)}, bf16[1024,512]{1,0:T(8,128)(2,1)S(1)}, u32[]{:S(2)}, u32[]{:S(2)}) collective-permute-start(bf16[1024,512]{1,0:T(8,128)(2,1)S(1)} %copy-done.47), channel_id=1, source_target_pairs={{0,8},{8,0},{16,24},{24,16},{1,9},{9,1},{17,25},{25,17},{2,10},{10... | collective-permute-start | bytes 3145736 | tf_op jit(solution)/shard_map/ppermute | solution.py:16
  157.0 64.0 %collective-permute-start.37 = (bf16[1024,512]{1,0:T(8,128)(2,1)}, bf16[1024,512]{1,0:T(8,128)(2,1)S(1)}, u32[]{:S(2)}, u32[]{:S(2)}) collective-permute-start(bf16[1024,512]{1,0:T(8,128)(2,1)} %collective-permute-done.33), channel_id=1, source_target_pairs={{0,16},{8,24},{16,0},{24,8},{1,17},{9,25},{17,1},{25,9},{2,18},{10... | collective-permute-start | bytes 3145736 | tf_op jit(solution)/shard_map/ppermute | solution.py:16
  176.1 77.7 %collective-permute-start.44 = (bf16[1024,512]{1,0:T(8,128)(2,1)S(1)}, bf16[1024,512]{1,0:T(8,128)(2,1)S(1)}, u32[]{:S(2)}, u32[]{:S(2)}) collective-permute-start(bf16[1024,512]{1,0:T(8,128)(2,1)S(1)} %copy-done.48), channel_id=1, source_target_pairs={{0,16},{8,24},{16,0},{24,8},{1,17},{9,25},{17,1},{25,9},{2,18},{10... | collective-permute-start | bytes 3145736 | tf_op jit(solution)/shard_map/ppermute | solution.py:16
  198.5 51.1 %collective-permute-start.54 = (bf16[320,1024]{1,0:T(8,128)(2,1)S(1)}, bf16[320,1024]{1,0:T(8,128)(2,1)S(1)}, u32[]{:S(2)}, u32[]{:S(2)}) collective-permute-start(bf16[320,1024]{1,0:T(8,128)(2,1)S(1)} %pad_maximum_fusion.3), channel_id=1, source_target_pairs={{0,1},{1,0},{2,3},{3,2},{4,5},{5,4},{6,7},{7,6},{8,9},{9,8},{10,11... | collective-permute-start | bytes 1966088 | tf_op jit(solution)/shard_map/ppermute | solution.py:16
  221.0 24.3 %collective-permute-start.38 = (bf16[1024,512]{1,0:T(8,128)(2,1)S(1)}, bf16[1024,512]{1,0:T(8,128)(2,1)S(1)}, u32[]{:S(2)}, u32[]{:S(2)}) collective-permute-start(bf16[1024,512]{1,0:T(8,128)(2,1)S(1)} %collective-permute-done.36), channel_id=1, source_target_pairs={{0,8},{8,0},{16,24},{24,16},{1,9},{9,1},{17,25},{25,17},{2,10},{10... | collective-permute-start | bytes 3145736 | tf_op jit(solution)/shard_map/ppermute | solution.py:16
  249.6 60.5 %collective-permute-start.42 = (bf16[1024,512]{1,0:T(8,128)(2,1)S(1)}, bf16[1024,512]{1,0:T(8,128)(2,1)S(1)}, u32[]{:S(2)}, u32[]{:S(2)}) collective-permute-start(bf16[1024,512]{1,0:T(8,128)(2,1)S(1)} %copy-done.48), channel_id=1, source_target_pairs={{0,8},{8,0},{16,24},{24,16},{1,9},{9,1},{17,25},{25,17},{2,10},{10... | collective-permute-start | bytes 3145736 | tf_op jit(solution)/shard_map/ppermute | solution.py:16
  252.9 64.5 %collective-permute-start.43 = (bf16[1024,512]{1,0:T(8,128)(2,1)S(1)}, bf16[1024,512]{1,0:T(8,128)(2,1)S(1)}, u32[]{:S(2)}, u32[]{:S(2)}) collective-permute-start(bf16[1024,512]{1,0:T(8,128)(2,1)S(1)} %copy-done.47), channel_id=1, source_target_pairs={{0,16},{8,24},{16,0},{24,8},{1,17},{9,25},{17,1},{25,9},{2,18},{10... | collective-permute-start | bytes 3145736 | tf_op jit(solution)/shard_map/ppermute | solution.py:16
  253.8 45.9 %collective-permute-start.45 = (bf16[1024,512]{1,0:T(8,128)(2,1)S(1)}, bf16[1024,512]{1,0:T(8,128)(2,1)S(1)}, u32[]{:S(2)}, u32[]{:S(2)}) collective-permute-start(bf16[1024,512]{1,0:T(8,128)(2,1)S(1)} %collective-permute-done.41), channel_id=1, source_target_pairs={{0,16},{8,24},{16,0},{24,8},{1,17},{9,25},{17,1},{25,9},{2,18},{10... | collective-permute-start | bytes 3145736 | tf_op jit(solution)/shard_map/ppermute | solution.py:16
  255.0 47.1 %collective-permute-start.46 = (bf16[1024,512]{1,0:T(8,128)(2,1)S(1)}, bf16[1024,512]{1,0:T(8,128)(2,1)S(1)}, u32[]{:S(2)}, u32[]{:S(2)}) collective-permute-start(bf16[1024,512]{1,0:T(8,128)(2,1)S(1)} %collective-permute-done.44), channel_id=1, source_target_pairs={{0,8},{8,0},{16,24},{24,16},{1,9},{9,1},{17,25},{25,17},{2,10},{10... | collective-permute-start | bytes 3145736 | tf_op jit(solution)/shard_map/ppermute | solution.py:16
  324.7 12.1 %collective-permute-start.55 = (bf16[320,1024]{1,0:T(8,128)(2,1)S(1)}, bf16[320,1024]{1,0:T(8,128)(2,1)S(1)}, u32[]{:S(2)}, u32[]{:S(2)}) collective-permute-start(bf16[320,1024]{1,0:T(8,128)(2,1)S(1)} %get-tuple-element.61), channel_id=1, source_target_pairs={{0,1},{1,0},{2,3},{3,2},{4,5},{5,4},{6,7},{7,6},{8,9},{9,8},{10,11... | collective-permute-start | bytes 1966088 | tf_op jit(solution)/shard_map/ppermute | solution.py:16
  324.8 12.1 %collective-permute-start.56 = (bf16[320,1024]{1,0:T(8,128)(2,1)S(1)}, bf16[320,1024]{1,0:T(8,128)(2,1)S(1)}, u32[]{:S(2)}, u32[]{:S(2)}) collective-permute-start(bf16[320,1024]{1,0:T(8,128)(2,1)S(1)} %get-tuple-element.62), channel_id=1, source_target_pairs={{0,1},{1,0},{2,3},{3,2},{4,5},{5,4},{6,7},{7,6},{8,9},{9,8},{10,11... | collective-permute-start | bytes 1966088 | tf_op jit(solution)/shard_map/ppermute | solution.py:16
  325.3 52.9 %collective-permute-start.100 = (bf16[1024,512]{1,0:T(8,128)(2,1)}, bf16[1024,512]{1,0:T(8,128)(2,1)}, u32[]{:S(2)}, u32[]{:S(2)}) collective-permute-start(bf16[1024,512]{1,0:T(8,128)(2,1)} %convolution_convert_fusion.1), channel_id=1, source_target_pairs={{0,16},{8,24},{16,0},{24,8},{1,17},{9,25},{17,1},{25,9},{2,18},{10... | collective-permute-start | bytes 3145736 | tf_op jit(solution)/shard_map/ppermute | solution.py:16
  326.1 48.8 %collective-permute-start.94 = (bf16[1024,512]{1,0:T(8,128)(2,1)S(1)}, bf16[1024,512]{1,0:T(8,128)(2,1)}, u32[]{:S(2)}, u32[]{:S(2)}) collective-permute-start(bf16[1024,512]{1,0:T(8,128)(2,1)S(1)} %copy-done.95), channel_id=1, source_target_pairs={{0,8},{8,0},{16,24},{24,16},{1,9},{9,1},{17,25},{25,17},{2,10},{10... | collective-permute-start | bytes 3145736 | tf_op jit(solution)/shard_map/ppermute | solution.py:16
  332.5 25.3 %collective-permute-start.47 = (bf16[320,1024]{1,0:T(8,128)(2,1)S(1)}, bf16[320,1024]{1,0:T(8,128)(2,1)S(1)}, u32[]{:S(2)}, u32[]{:S(2)}) collective-permute-start(bf16[320,1024]{1,0:T(8,128)(2,1)S(1)} %slice.510), channel_id=1, source_target_pairs={{0,1},{1,0},{2,3},{3,2},{4,5},{5,4},{6,7},{7,6},{8,9},{9,8},{10,11... | collective-permute-start | bytes 1966088 | tf_op jit(solution)/shard_map/ppermute | solution.py:16
  358.4 14.6 %collective-permute-start.49 = (bf16[80,1024]{1,0:T(8,128)(2,1)S(1)}, bf16[80,1024]{1,0:T(8,128)(2,1)S(1)}, u32[]{:S(2)}, u32[]{:S(2)}) collective-permute-start(bf16[80,1024]{1,0:T(8,128)(2,1)S(1)} %get-tuple-element.76), channel_id=1, source_target_pairs={{0,4},{1,5},{2,6},{3,7},{4,0},{5,1},{6,2},{7,3},{8,12},{9,13},{10,... | collective-permute-start | bytes 491528 | tf_op jit(solution)/shard_map/ppermute | solution.py:40
  358.5 15.1 %collective-permute-start.50 = (bf16[80,1024]{1,0:T(8,128)(2,1)S(1)}, bf16[80,1024]{1,0:T(8,128)(2,1)S(1)}, u32[]{:S(2)}, u32[]{:S(2)}) collective-permute-start(bf16[80,1024]{1,0:T(8,128)(2,1)S(1)} %get-tuple-element.75), channel_id=1, source_target_pairs={{0,2},{1,3},{2,4},{3,5},{4,6},{5,7},{6,0},{7,1},{8,10},{9,11},{10,... | collective-permute-start | bytes 491528 | tf_op jit(solution)/shard_map/ppermute | solution.py:40
  366.1 109.7 %collective-permute-start.97 = (bf16[1024,512]{1,0:T(8,128)(2,1)}, bf16[1024,512]{1,0:T(8,128)(2,1)}, u32[]{:S(2)}, u32[]{:S(2)}) collective-permute-start(bf16[1024,512]{1,0:T(8,128)(2,1)} %convolution_convert_fusion.3), channel_id=1, source_target_pairs={{0,16},{8,24},{16,0},{24,8},{1,17},{9,25},{17,1},{25,9},{2,18},{10... | collective-permute-start | bytes 3145736 | tf_op jit(solution)/shard_map/ppermute | solution.py:16
  373.0 124.9 %collective-permute-start.91 = (bf16[1024,512]{1,0:T(8,128)(2,1)}, bf16[1024,512]{1,0:T(8,128)(2,1)}, u32[]{:S(2)}, u32[]{:S(2)}) collective-permute-start(bf16[1024,512]{1,0:T(8,128)(2,1)} %convolution_convert_fusion.7), channel_id=1, source_target_pairs={{0,8},{8,0},{16,24},{24,16},{1,9},{9,1},{17,25},{25,17},{2,10},{10... | collective-permute-start | bytes 3145736 | tf_op jit(solution)/shard_map/ppermute | solution.py:16
  383.5 17.4 %collective-permute-start.59 = (bf16[80,1024]{1,0:T(8,128)(2,1)S(1)}, bf16[80,1024]{1,0:T(8,128)(2,1)S(1)}, u32[]{:S(2)}, u32[]{:S(2)}) collective-permute-start(bf16[80,1024]{1,0:T(8,128)(2,1)S(1)} %get-tuple-element.67), channel_id=1, source_target_pairs={{0,4},{1,5},{2,6},{3,7},{4,0},{5,1},{6,2},{7,3},{8,12},{9,13},{10,... | collective-permute-start | bytes 491528 | tf_op jit(solution)/shard_map/ppermute | solution.py:40
  385.8 15.2 %collective-permute-start.60 = (bf16[80,1024]{1,0:T(8,128)(2,1)S(1)}, bf16[80,1024]{1,0:T(8,128)(2,1)S(1)}, u32[]{:S(2)}, u32[]{:S(2)}) collective-permute-start(bf16[80,1024]{1,0:T(8,128)(2,1)S(1)} %get-tuple-element.66), channel_id=1, source_target_pairs={{0,2},{1,3},{2,4},{3,5},{4,6},{5,7},{6,0},{7,1},{8,10},{9,11},{10,... | collective-permute-start | bytes 491528 | tf_op jit(solution)/shard_map/ppermute | solution.py:40
  416.3 64.7 %collective-permute-start.80 = (bf16[4,32,1024]{2,1,0:T(8,128)(2,1)}, bf16[4,32,1024]{2,1,0:T(8,128)(2,1)}, u32[]{:S(2)}, u32[]{:S(2)}) collective-permute-start(bf16[4,32,1024]{2,1,0:T(8,128)(2,1)} %fusion.133), channel_id=1, source_target_pairs={{0,1},{1,0},{2,3},{3,2},{4,5},{5,4},{6,7},{7,6},{8,9},{9,8},{10,11... | collective-permute-start | bytes 786440 | tf_op jit(solution)/shard_map/ppermute | solution.py:16
  416.3 62.5 %collective-permute-start.81 = (bf16[4,32,1024]{2,1,0:T(8,128)(2,1)}, bf16[4,32,1024]{2,1,0:T(8,128)(2,1)}, u32[]{:S(2)}, u32[]{:S(2)}) collective-permute-start(bf16[4,32,1024]{2,1,0:T(8,128)(2,1)} %fusion.134), channel_id=1, source_target_pairs={{0,1},{1,0},{2,3},{3,2},{4,5},{5,4},{6,7},{7,6},{8,9},{9,8},{10,11... | collective-permute-start | bytes 786440 | tf_op jit(solution)/shard_map/ppermute | solution.py:16
  416.8 66.2 %collective-permute-start.78 = (bf16[4,32,1024]{2,1,0:T(8,128)(2,1)}, bf16[4,32,1024]{2,1,0:T(8,128)(2,1)}, u32[]{:S(2)}, u32[]{:S(2)}) collective-permute-start(bf16[4,32,1024]{2,1,0:T(8,128)(2,1)} %fusion.132), channel_id=1, source_target_pairs={{0,1},{1,0},{2,3},{3,2},{4,5},{5,4},{6,7},{7,6},{8,9},{9,8},{10,11... | collective-permute-start | bytes 786440 | tf_op jit(solution)/shard_map/ppermute | solution.py:16
  475.9 15.3 %collective-permute-start.77 = (bf16[4,32,1024]{2,1,0:T(8,128)(2,1)S(1)}, bf16[4,32,1024]{2,1,0:T(8,128)(2,1)S(1)}, u32[]{:S(2)}, u32[]{:S(2)}) collective-permute-start(bf16[4,32,1024]{2,1,0:T(8,128)(2,1)S(1)} %copy-done.70), channel_id=1, source_target_pairs={{0,1},{1,0},{2,3},{3,2},{4,5},{5,4},{6,7},{7,6},{8,9},{9,8},{10,11... | collective-permute-start | bytes 786440 | tf_op jit(solution)/shard_map/ppermute | solution.py:16
  492.5 39.5 %collective-permute-start.99 = (bf16[1024,512]{1,0:T(8,128)(2,1)S(1)}, bf16[1024,512]{1,0:T(8,128)(2,1)S(1)}, u32[]{:S(2)}, u32[]{:S(2)}) collective-permute-start(bf16[1024,512]{1,0:T(8,128)(2,1)S(1)} %copy-done.88), channel_id=1, source_target_pairs={{0,16},{8,24},{16,0},{24,8},{1,17},{9,25},{17,1},{25,9},{2,18},{10... | collective-permute-start | bytes 3145736 | tf_op jit(solution)/shard_map/ppermute | solution.py:16
  493.8 39.4 %collective-permute-start.101 = (bf16[1024,512]{1,0:T(8,128)(2,1)S(1)}, bf16[1024,512]{1,0:T(8,128)(2,1)S(1)}, u32[]{:S(2)}, u32[]{:S(2)}) collective-permute-start(bf16[1024,512]{1,0:T(8,128)(2,1)S(1)} %copy-done.90), channel_id=1, source_target_pairs={{0,8},{8,0},{16,24},{24,16},{1,9},{9,1},{17,25},{25,17},{2,10},{10... | collective-permute-start | bytes 3145736 | tf_op jit(solution)/shard_map/ppermute | solution.py:16
  496.7 27.4 %collective-permute-start.65 = (bf16[128,1024]{1,0:T(8,128)(2,1)S(1)}, bf16[128,1024]{1,0:T(8,128)(2,1)S(1)}, u32[]{:S(2)}, u32[]{:S(2)}) collective-permute-start(bf16[128,1024]{1,0:T(8,128)(2,1)S(1)} %get-tuple-element.48), channel_id=1, source_target_pairs={{0,8},{8,0},{16,24},{24,16},{1,9},{9,1},{17,25},{25,17},{2,10},{10... | collective-permute-start | bytes 786440 | tf_op jit(solution)/shard_map/ppermute | solution.py:16
  497.9 27.2 %collective-permute-start.87 = (bf16[32,1024]{1,0:T(8,128)(2,1)S(1)}, bf16[32,1024]{1,0:T(8,128)(2,1)S(1)}, u32[]{:S(2)}, u32[]{:S(2)}) collective-permute-start(bf16[32,1024]{1,0:T(8,128)(2,1)S(1)} %get-tuple-element.83), channel_id=1, source_target_pairs={{0,2},{1,3},{2,4},{3,5},{4,6},{5,7},{6,0},{7,1},{8,10},{9,11},{10,... | collective-permute-start | bytes 196616 | tf_op jit(solution)/shard_map/ppermute | solution.py:40
  498.0 27.9 %collective-permute-start.88 = (bf16[32,1024]{1,0:T(8,128)(2,1)S(1)}, bf16[32,1024]{1,0:T(8,128)(2,1)S(1)}, u32[]{:S(2)}, u32[]{:S(2)}) collective-permute-start(bf16[32,1024]{1,0:T(8,128)(2,1)S(1)} %get-tuple-element.84), channel_id=1, source_target_pairs={{0,4},{1,5},{2,6},{3,7},{4,0},{5,1},{6,2},{7,3},{8,12},{9,13},{10,... | collective-permute-start | bytes 196616 | tf_op jit(solution)/shard_map/ppermute | solution.py:40
  524.1 38.5 %collective-permute-start.93 = (bf16[1024,512]{1,0:T(8,128)(2,1)S(1)}, bf16[1024,512]{1,0:T(8,128)(2,1)S(1)}, u32[]{:S(2)}, u32[]{:S(2)}) collective-permute-start(bf16[1024,512]{1,0:T(8,128)(2,1)S(1)} %copy-done.87), channel_id=1, source_target_pairs={{0,8},{8,0},{16,24},{24,16},{1,9},{9,1},{17,25},{25,17},{2,10},{10... | collective-permute-start | bytes 3145736 | tf_op jit(solution)/shard_map/ppermute | solution.py:16
  525.1 38.4 %collective-permute-start.95 = (bf16[1024,512]{1,0:T(8,128)(2,1)S(1)}, bf16[1024,512]{1,0:T(8,128)(2,1)S(1)}, u32[]{:S(2)}, u32[]{:S(2)}) collective-permute-start(bf16[1024,512]{1,0:T(8,128)(2,1)S(1)} %copy-done.89), channel_id=1, source_target_pairs={{0,16},{8,24},{16,0},{24,8},{1,17},{9,25},{17,1},{25,9},{2,18},{10... | collective-permute-start | bytes 3145736 | tf_op jit(solution)/shard_map/ppermute | solution.py:16
  530.2 23.1 %collective-permute-start.64 = (bf16[128,1024]{1,0:T(8,128)(2,1)S(1)}, bf16[128,1024]{1,0:T(8,128)(2,1)S(1)}, u32[]{:S(2)}, u32[]{:S(2)}) collective-permute-start(bf16[128,1024]{1,0:T(8,128)(2,1)S(1)} %get-tuple-element.45), channel_id=1, source_target_pairs={{0,8},{8,0},{16,24},{24,16},{1,9},{9,1},{17,25},{25,17},{2,10},{10... | collective-permute-start | bytes 786440 | tf_op jit(solution)/shard_map/ppermute | solution.py:16
  531.9 24.9 %collective-permute-start.68 = (bf16[128,1024]{1,0:T(8,128)(2,1)S(1)}, bf16[128,1024]{1,0:T(8,128)(2,1)S(1)}, u32[]{:S(2)}, u32[]{:S(2)}) collective-permute-start(bf16[128,1024]{1,0:T(8,128)(2,1)S(1)} %get-tuple-element.46), channel_id=1, source_target_pairs={{0,16},{8,24},{16,0},{24,8},{1,17},{9,25},{17,1},{25,9},{2,18},{10... | collective-permute-start | bytes 786440 | tf_op jit(solution)/shard_map/ppermute | solution.py:16
  533.1 29.3 %collective-permute-start.66 = (bf16[128,1024]{1,0:T(8,128)(2,1)S(1)}, bf16[128,1024]{1,0:T(8,128)(2,1)S(1)}, u32[]{:S(2)}, u32[]{:S(2)}) collective-permute-start(bf16[128,1024]{1,0:T(8,128)(2,1)S(1)} %fusion.116), channel_id=1, source_target_pairs={{0,16},{8,24},{16,0},{24,8},{1,17},{9,25},{17,1},{25,9},{2,18},{10... | collective-permute-start | bytes 786440 | tf_op jit(solution)/shard_map/ppermute | solution.py:16
  553.2 61.0 %collective-permute-start.96 = (bf16[1024,512]{1,0:T(8,128)(2,1)S(1)}, bf16[1024,512]{1,0:T(8,128)(2,1)S(1)}, u32[]{:S(2)}, u32[]{:S(2)}) collective-permute-start(bf16[1024,512]{1,0:T(8,128)(2,1)S(1)} %copy-done.85), channel_id=1, source_target_pairs={{0,16},{8,24},{16,0},{24,8},{1,17},{9,25},{17,1},{25,9},{2,18},{10... | collective-permute-start | bytes 3145736 | tf_op jit(solution)/shard_map/ppermute | solution.py:16
  556.8 63.0 %collective-permute-start.90 = (bf16[1024,512]{1,0:T(8,128)(2,1)S(1)}, bf16[1024,512]{1,0:T(8,128)(2,1)S(1)}, u32[]{:S(2)}, u32[]{:S(2)}) collective-permute-start(bf16[1024,512]{1,0:T(8,128)(2,1)S(1)} %copy-done.86), channel_id=1, source_target_pairs={{0,8},{8,0},{16,24},{24,16},{1,9},{9,1},{17,25},{25,17},{2,10},{10... | collective-permute-start | bytes 3145736 | tf_op jit(solution)/shard_map/ppermute | solution.py:16
  562.4 26.7 %collective-permute-start.70 = (bf16[4,4,32,896]{3,2,0,1:T(8,128)(2,1)S(1)}, bf16[4,4,32,896]{3,2,0,1:T(8,128)(2,1)S(1)}, u32[]{:S(2)}, u32[]{:S(2)}) collective-permute-start(bf16[4,4,32,896]{3,2,0,1:T(8,128)(2,1)S(1)} %fusion.93), channel_id=1, source_target_pairs={{0,1},{1,0},{2,3},{3,2},{4,5},{5,4},{6,7},{7,6},{8,9},{9,8},{10,11... | collective-permute-start | bytes 2752520 | tf_op jit(solution)/shard_map/ppermute | solution.py:16
  562.6 25.0 %collective-permute-start.67 = (bf16[128,1024]{1,0:T(8,128)(2,1)S(1)}, bf16[128,1024]{1,0:T(8,128)(2,1)S(1)}, u32[]{:S(2)}, u32[]{:S(2)}) collective-permute-start(bf16[128,1024]{1,0:T(8,128)(2,1)S(1)} %get-tuple-element.47), channel_id=1, source_target_pairs={{0,16},{8,24},{16,0},{24,8},{1,17},{9,25},{17,1},{25,9},{2,18},{10... | collective-permute-start | bytes 786440 | tf_op jit(solution)/shard_map/ppermute | solution.py:16
  563.5 25.2 %collective-permute-start.69 = (bf16[128,1024]{1,0:T(8,128)(2,1)S(1)}, bf16[128,1024]{1,0:T(8,128)(2,1)S(1)}, u32[]{:S(2)}, u32[]{:S(2)}) collective-permute-start(bf16[128,1024]{1,0:T(8,128)(2,1)S(1)} %get-tuple-element.43), channel_id=1, source_target_pairs={{0,8},{8,0},{16,24},{24,16},{1,9},{9,1},{17,25},{25,17},{2,10},{10... | collective-permute-start | bytes 786440 | tf_op jit(solution)/shard_map/ppermute | solution.py:16
  587.6 26.6 %collective-permute-start.98 = (bf16[1024,512]{1,0:T(8,128)(2,1)S(1)}, bf16[1024,512]{1,0:T(8,128)(2,1)S(1)}, u32[]{:S(2)}, u32[]{:S(2)}) collective-permute-start(bf16[1024,512]{1,0:T(8,128)(2,1)S(1)} %add_convert_fusion.2), channel_id=1, source_target_pairs={{0,8},{8,0},{16,24},{24,16},{1,9},{9,1},{17,25},{25,17},{2,10},{10... | collective-permute-start | bytes 3145736 | tf_op jit(solution)/shard_map/ppermute | solution.py:16
  591.2 15.7 %collective-permute-start.72 = (bf16[4,32,896]{2,1,0:T(8,128)(2,1)S(1)}, bf16[4,32,896]{2,1,0:T(8,128)(2,1)S(1)}, u32[]{:S(2)}, u32[]{:S(2)}) collective-permute-start(bf16[4,32,896]{2,1,0:T(8,128)(2,1)S(1)} %get-tuple-element.55), channel_id=1, source_target_pairs={{0,4},{1,5},{2,6},{3,7},{4,0},{5,1},{6,2},{7,3},{8,12},{9,13},{10,... | collective-permute-start | bytes 688136 | tf_op jit(solution)/shard_map/ppermute | solution.py:40
  600.0 21.8 %collective-permute-start.92 = (bf16[1024,512]{1,0:T(8,128)(2,1)S(1)}, bf16[1024,512]{1,0:T(8,128)(2,1)S(1)}, u32[]{:S(2)}, u32[]{:S(2)}) collective-permute-start(bf16[1024,512]{1,0:T(8,128)(2,1)S(1)} %add_convert_fusion.4), channel_id=1, source_target_pairs={{0,16},{8,24},{16,0},{24,8},{1,17},{9,25},{17,1},{25,9},{2,18},{10... | collective-permute-start | bytes 3145736 | tf_op jit(solution)/shard_map/ppermute | solution.py:16
  613.3 11.5 %collective-permute-start.74 = (bf16[32,896]{1,0:T(8,128)(2,1)S(1)}, bf16[32,896]{1,0:T(8,128)(2,1)S(1)}, u32[]{:S(2)}, u32[]{:S(2)}) collective-permute-start(bf16[32,896]{1,0:T(8,128)(2,1)S(1)} %get-tuple-element.113), channel_id=1, source_target_pairs={{0,8},{8,0},{16,24},{24,16},{1,9},{9,1},{17,25},{25,17},{2,10},{10... | collective-permute-start | bytes 172040 | tf_op jit(solution)/shard_map/ppermute | solution.py:16
  614.2 10.5 %collective-permute-start.75 = (bf16[32,896]{1,0:T(8,128)(2,1)S(1)}, bf16[32,896]{1,0:T(8,128)(2,1)S(1)}, u32[]{:S(2)}, u32[]{:S(2)}) collective-permute-start(bf16[32,896]{1,0:T(8,128)(2,1)S(1)} %get-tuple-element.112), channel_id=1, source_target_pairs={{0,16},{8,24},{16,0},{24,8},{1,17},{9,25},{17,1},{25,9},{2,18},{10... | collective-permute-start | bytes 172040 | tf_op jit(solution)/shard_map/ppermute | solution.py:16
  (156 other events, 1739.6 us)
